TPU v7x, 32 devices: a whole 2x2x4 slice. The times are simulated.
32 devices in a mesh: dp: 4 (over y, x), blk: 8 (over z, core).
Axes of the slice: x: 2, y: 2, z: 4, core: 2. Of those that a mesh axis runs over, the one named last changes fastest.
Arguments:
- tokens: bfloat16 [8, 1024, 768], P('dp', 'blk'), may hold values from -6 to 6
- segment_ids: int32 [8, 1024], P('dp', 'blk'), may hold values from 0 to 5, never falling along the last dimension, each value on 1 to 512 neighbouring positions
- gain_attn: bfloat16 [768], replicated, may hold values from 0.5 to 1.5
- w_query: bfloat16 [768, 768], replicated, may hold values from -0.109375 to 0.109375
- w_key: bfloat16 [768, 768], replicated, may hold values from -0.109375 to 0.109375
- w_value: bfloat16 [768, 768], replicated, may hold values from -0.21875 to 0.21875
- w_out: bfloat16 [768, 768], replicated, may hold values from -0.875 to 0.875
- gain_ffn: bfloat16 [768], replicated, may hold values from 0.5 to 1.5
- w_in: bfloat16 [768, 3072], replicated, may hold values from -0.21875 to 0.21875
- w_down: bfloat16 [3072, 768], replicated, may hold values from -0.15625 to 0.15625
- rel_table: bfloat16 [32, 12], replicated, may hold values from -4 to 4
- cotangent: bfloat16 [8, 1024, 768], P('dp', 'blk'), may hold values from -6 to 6
Outputs:
- output: bfloat16 [8, 1024, 768], P('dp', 'blk')
- grad_tokens: bfloat16 [8, 1024, 768], P('dp', 'blk')
- grad_gain_attn: float32 [768], P('blk')
- grad_w_query: float32 [768, 768], P('blk')
- grad_w_key: float32 [768, 768], P('blk')
- grad_w_value: float32 [768, 768], P('blk')
- grad_w_out: float32 [768, 768], P('blk')
- grad_gain_ffn: float32 [768], P('blk')
- grad_w_in: float32 [768, 3072], P('blk')
- grad_w_down: float32 [3072, 768], P('blk')
- grad_rel_table: float32 [32, 12], P('blk')
Inputs may be any that keep to these rules, and one draw needn't show every extreme that they name: `segment_ids`: along each row of 1024 positions the ids never fall, so each id covers one contiguous run of tokens, a sequence of at most 512 tokens; a token attends only to tokens of its row with its id.
All inputs are finite; a program needn't handle non-finite values.
Results may differ from a plain program's by a relative error of at most 0.014.
The roundings to bfloat16 on the way count: a program that leaves them out, or rounds other values in their place, can miss the bound.
Values may be sent and summed in bfloat16 or wider, within the bound.
A program may use at most 192 MiB of HBM per device.

v0:
```python
import math

import jax
import jax.numpy as jnp
from jax import lax
from jax.sharding import PartitionSpec as P

EPS = 1e-06
NEG = -1e30
EDGES = (12, 16, 23, 32, 46, 64, 91)
ROOT_TWO_PI = 0.7978845608028654
CUBIC = 0.044715


def bucket_of(offset):
    distance = jnp.abs(offset)
    far_part = 8 + sum(((distance >= edge).astype(jnp.int32) for edge in EDGES))
    return jnp.where(offset > 0, 16, 0) + jnp.where(distance < 8, distance, far_part)


def gelu_both(values):
    inner_arg = ROOT_TWO_PI * (values + CUBIC * values * values * values)
    tangent = jnp.tanh(inner_arg)
    result = 0.5 * values * (1.0 + tangent)
    slope = 0.5 * (1.0 + tangent) + 0.5 * values * (1.0 - tangent * tangent) * ROOT_TWO_PI * (
        1.0 + 3.0 * CUBIC * values * values
    )
    return (result, slope)


def rms_forward(values, gain):
    scale = lax.rsqrt(jnp.mean(values * values, axis=-1, keepdims=True) + EPS)
    normed = values * scale
    return (normed, scale, (normed * gain).astype(jnp.bfloat16))


def rms_backward(grad, normed, scale, gain):
    gain_grad = jnp.sum(grad * normed, axis=0)
    inner_grad = grad * gain
    back = scale * (inner_grad - normed * jnp.mean(inner_grad * normed, axis=-1, keepdims=True))
    return (back, gain_grad)


def outer_sum(left, right):
    return jnp.einsum("td,tf->df", left, right, preferred_element_type=jnp.float32)


def times_t(left, right):
    return jnp.einsum("tf,df->td", left, right, preferred_element_type=jnp.float32)


def masked_scores(query, keys, bias, seg_query, seg_keys):
    raw = (
        jnp.einsum("bqhd,bkhd->bhqk", query, keys, preferred_element_type=jnp.float32) + bias[None]
    )
    same = seg_query[:, None, :, None] == seg_keys[:, None, None, :]
    return jnp.where(same, raw, NEG)


def score_grads(q_part, k_part, v_part, bias, sq_part, sk_part, total, d_mixed):
    scores = masked_scores(q_part, k_part, bias, sq_part, sk_part)
    probs = jnp.exp(scores - total[..., None])
    grad_probs = jnp.einsum("bqhd,bkhd->bhqk", d_mixed, v_part, preferred_element_type=jnp.float32)
    return (probs, grad_probs)


def on_device(
    tokens,
    segment_ids,
    gain_attn,
    w_query,
    w_key,
    w_value,
    w_out,
    gain_ffn,
    w_in,
    w_down,
    rel_table,
    cotangent,
):
    rows, block, width = tokens.shape
    buckets, heads = rel_table.shape
    inner = w_query.shape[1]
    head_dim = inner // heads
    length = block * lax.axis_size("blk")
    group = math.gcd(rows, max(1, 512 // block))
    blocks = rows // group
    gain_one = gain_attn.astype(jnp.float32)
    gain_two = gain_ffn.astype(jnp.float32)
    table_f = rel_table.astype(jnp.float32)
    flat = tokens.reshape(rows * block, width).astype(jnp.float32)
    normed_one, scale_one, low_one = rms_forward(flat, gain_one)

    def project(weight):
        return (
            jnp.dot(low_one, weight, preferred_element_type=jnp.float32)
            .astype(jnp.bfloat16)
            .reshape(rows, block, inner)
        )

    query, keys, values = (project(w_query), project(w_key), project(w_value))
    key_all, value_all, seg_all = (
        lax.all_gather(keys, "blk", axis=1, tiled=True),
        lax.all_gather(values, "blk", axis=1, tiled=True),
        lax.all_gather(segment_ids, "blk", axis=1, tiled=True),
    )
    places = lax.axis_index("blk") * block + jnp.arange(block, dtype=jnp.int32)
    offsets = jnp.arange(length, dtype=jnp.int32)[None, :] - places[:, None]
    onehot = (
        bucket_of(offsets)[None] == jnp.arange(buckets, dtype=jnp.int32)[:, None, None]
    ).astype(jnp.float32)
    bias = jnp.einsum("nqk,nh->hqk", onehot, table_f, precision=lax.Precision.HIGHEST)
    q_groups = query.reshape(blocks, group, block, heads, head_dim)
    seg_query = segment_ids.reshape(blocks, group, block)

    def key_groups(key_rows, value_rows, seg_rows):
        return (
            key_rows.reshape(blocks, group, length, heads, head_dim),
            value_rows.reshape(blocks, group, length, heads, head_dim),
            seg_rows.reshape(blocks, group, length),
        )

    k_groups, v_groups, seg_keys = key_groups(key_all, value_all, seg_all)

    def attend(parts):
        q_part, k_part, v_part, sq_part, sk_part = parts
        scores = masked_scores(q_part, k_part, bias, sq_part, sk_part)
        top = jnp.max(scores, axis=-1, keepdims=True)
        total = jnp.log(jnp.sum(jnp.exp(scores - top), axis=-1, keepdims=True)) + top
        probs = jnp.exp(scores - total).astype(jnp.bfloat16)
        mixed = jnp.einsum("bhqk,bkhd->bqhd", probs, v_part, preferred_element_type=jnp.float32)
        return (mixed.astype(jnp.bfloat16), total[..., 0])

    attended, log_totals = lax.map(attend, (q_groups, k_groups, v_groups, seg_query, seg_keys))
    attended_flat = attended.reshape(rows * block, inner)
    hidden = flat + jnp.dot(attended_flat, w_out, preferred_element_type=jnp.float32)
    normed_two, scale_two, low_two = rms_forward(hidden, gain_two)
    pre = jnp.dot(low_two, w_in, preferred_element_type=jnp.float32)
    gelu_value, gelu_slope = gelu_both(pre)
    active = gelu_value.astype(jnp.bfloat16)
    output = (hidden + jnp.dot(active, w_down, preferred_element_type=jnp.float32)).astype(
        jnp.bfloat16
    )
    grad_out = cotangent.reshape(rows * block, width)
    grad_down = outer_sum(active, grad_out)
    grad_pre = (times_t(grad_out, w_down) * gelu_slope).astype(jnp.bfloat16)
    grad_in = outer_sum(low_two, grad_pre)
    back_two, grad_gain_two = rms_backward(times_t(grad_pre, w_in), normed_two, scale_two, gain_two)
    grad_hidden = grad_out.astype(jnp.float32) + back_two
    grad_proj = grad_hidden.astype(jnp.bfloat16)
    grad_wout = outer_sum(attended_flat, grad_proj)
    grad_att = (
        times_t(grad_proj, w_out)
        .astype(jnp.bfloat16)
        .reshape(blocks, group, block, heads, head_dim)
    )
    key_back, value_back, seg_back = (
        lax.all_gather(keys, "blk", axis=1, tiled=True),
        lax.all_gather(values, "blk", axis=1, tiled=True),
        lax.all_gather(segment_ids, "blk", axis=1, tiled=True),
    )
    k_back, v_back, sk_back = key_groups(key_back, value_back, seg_back)
    start = jnp.zeros((heads, block, length), jnp.float32)

    def attend_back(carry, parts):
        q_part, k_part, v_part, sq_part, sk_part, total, d_mixed = parts
        probs, grad_probs = score_grads(
            q_part, k_part, v_part, bias, sq_part, sk_part, total, d_mixed
        )
        center = jnp.sum(probs * grad_probs, axis=-1, keepdims=True)
        grad_scores = (probs * (grad_probs - center)).astype(jnp.bfloat16)
        grad_q = jnp.einsum(
            "bhqk,bkhd->bqhd", grad_scores, k_part, preferred_element_type=jnp.float32
        ).astype(jnp.bfloat16)
        grad_k = jnp.einsum(
            "bhqk,bqhd->bkhd", grad_scores, q_part, preferred_element_type=jnp.float32
        )
        grad_v = jnp.einsum(
            "bhqk,bqhd->bkhd",
            probs.astype(jnp.bfloat16),
            d_mixed,
            preferred_element_type=jnp.float32,
        )
        paired = jnp.stack([grad_k, grad_v], axis=2).reshape(group, length, 2, inner)
        return (carry + jnp.sum(grad_scores.astype(jnp.float32), axis=0), (grad_q, paired))

    bias_grad, (grad_query, paired) = lax.scan(
        attend_back, start, (q_groups, k_back, v_back, seg_query, sk_back, log_totals, grad_att)
    )
    paired = paired.reshape(rows, length, 2, inner)
    kv_grad = lax.psum_scatter(paired, "blk", scatter_dimension=1, tiled=True).astype(jnp.bfloat16)
    grad_key = kv_grad[:, :, 0].reshape(rows * block, inner)
    grad_value = kv_grad[:, :, 1].reshape(rows * block, inner)
    grad_query = grad_query.reshape(rows * block, inner)
    grad_wq = outer_sum(low_one, grad_query)
    grad_wk = outer_sum(low_one, grad_key)
    grad_wv = outer_sum(low_one, grad_value)
    grad_low_one = (
        times_t(grad_query, w_query) + times_t(grad_key, w_key) + times_t(grad_value, w_value)
    )
    back_one, grad_gain_one = rms_backward(grad_low_one, normed_one, scale_one, gain_one)
    grad_tokens = (grad_hidden + back_one).astype(jnp.bfloat16).reshape(rows, block, width)
    grad_table = jnp.einsum("hqk,nqk->nh", bias_grad, onehot, precision=lax.Precision.HIGHEST)
    grads = (
        grad_gain_one,
        grad_wq,
        grad_wk,
        grad_wv,
        grad_wout,
        grad_gain_two,
        grad_in,
        grad_down,
        grad_table,
    )
    pieces = (
        lax.psum_scatter(grads[0], "blk", scatter_dimension=0, tiled=True),
        lax.psum_scatter(grads[1], "blk", scatter_dimension=0, tiled=True),
        lax.psum_scatter(grads[2], "blk", scatter_dimension=0, tiled=True),
        lax.psum_scatter(grads[3], "blk", scatter_dimension=0, tiled=True),
        lax.psum_scatter(grads[4], "blk", scatter_dimension=0, tiled=True),
        lax.psum_scatter(grads[5], "blk", scatter_dimension=0, tiled=True),
        lax.psum_scatter(grads[6], "blk", scatter_dimension=0, tiled=True),
        lax.psum_scatter(grads[7], "blk", scatter_dimension=0, tiled=True),
        lax.psum_scatter(grads[8], "blk", scatter_dimension=0, tiled=True),
    )
    shares = lax.psum(
        (
            pieces[0],
            pieces[1],
            pieces[2],
            pieces[3],
            pieces[4],
            pieces[5],
            pieces[6],
            pieces[7],
            pieces[8],
        ),
        "dp",
    )
    return (
        output.reshape(rows, block, width),
        grad_tokens,
        shares[0],
        shares[1],
        shares[2],
        shares[3],
        shares[4],
        shares[5],
        shares[6],
        shares[7],
        shares[8],
    )


def solution(mesh):
    placed = (
        P("dp", "blk", None),
        P("dp", "blk"),
        P(),
        P(),
        P(),
        P(),
        P(),
        P(),
        P(),
        P(),
        P(),
        P("dp", "blk", None),
    )
    return jax.shard_map(
        on_device,
        mesh=mesh,
        in_specs=placed,
        out_specs=(
            P("dp", "blk", None),
            P("dp", "blk", None),
            P("blk"),
            P("blk", None),
            P("blk", None),
            P("blk", None),
            P("blk", None),
            P("blk"),
            P("blk", None),
            P("blk", None),
            P("blk", None),
        ),
        check_vma=False,
    )
```

profile of v0, /device:TPU:3, one launch (start us, length us, event | category | flops | bytes accessed | tf_op | source)
XLA Modules:
  0.0 811.9 jit_solution(4157759957743839460)
XLA Ops:
  18.6 74.4 %copy.49 = pred[32,128,1024]{2,0,1:T(32,128)(4,1)S(1)} copy(pred[32,128,1024]{1,0,2:T(32,128)(4,1)S(1)} %iota_compare_fusion) | data formatting | bytes 8388608 | tf_op jit(solution)/shard_map/eq | solution.py:110
  95.1 6.3 copy.50
  101.4 12.9 %all_gather.13 = s32[2,1024]{1,0:T(2,128)S(1)} all-gather(s32[2,128]{1,0:T(2,128)S(1)} %copy-done.36), channel_id=1, replica_groups=mesh['dp'=4,'blk'=8] {'blk'}, dimensions={1}, use_global_device_ids=true | all-gather | bytes 9216 | tf_op jit(solution)/shard_map/all_gather | solution.py:105
  159.5 6.7 fusion.32
  166.2 11.0 %multiply_reduce_fusion = (f32[2,12,128]{2,1,0:T(8,128)}, f32[2,12,128,1024]{3,2,1,0:T(8,128)}) fusion(f32[2,12,128,1024]{3,2,1,0:T(8,128)} %copy-done.1, f32[2,12,128]{2,1,0:T(8,128)S(1)} %copy-done.32, f32[12,128,1024]{2,1,0:T(8,128)S(1)} %bitcast.105, pred[2,128,1024]{2,1,0:T(8,128)(4,1)S(1)} %broadcast_compare_fusion, ...), kind=kOutput, calls=%fused_computation.4 | convolution fusion | flops 418378752 | bytes 35282944 | tf_op jit(solution)/shard_map/while/body/eval_jaxpr/bqhd,bkhd->bhqk/dot_general | solution.py:63
  177.2 6.6 copy.58
  183.9 14.7 %convert_reduce_fusion = (f32[12,128,1024]{2,1,0:T(8,128)}, bf16[2,12,128,1024]{3,2,1,0:T(8,128)(2,1)S(1)}) fusion(f32[2,12,128,1024]{3,2,1,0:T(8,128)} %get-tuple-element.102, f32[2,12,128]{2,1,0:T(8,128)S(1)} %copy-done.34, f32[2,12,128]{2,1,0:T(8,128)S(1)} %copy-done.33, f32[2,12,128,1024]{3,2,1,0:T(8,128)} %copy-done.1, f32[12,128,1024]{2,1,0:T(8,128)} %copy.50, ...), kind=kLoop, calls=%fused_computation.2 | loop fusion | flops 23592960 | bytes 44326912 | tf_op jit(solution)/shard_map/while/body/eval_jaxpr/reduce_sum | solution.py:185
  203.2 6.6 copy.57
  209.8 10.4 %pad_maximum_fusion = f32[2,1024,2,768]{3,1,0,2:T(8,128)} fusion(f32[2,1024,1,768]{3,1,0,2:T(8,128)} %copy.58, f32[2,1024,1,768]{3,1,0,2:T(8,128)} %copy.57), kind=kLoop, calls=%fused_computation.1 | loop fusion | flops 3145728 | bytes 25165824 | tf_op jit(solution)/shard_map/while/body/eval_jaxpr/stack | solution.py:184
  223.8 7.1 fusion.10
  233.5 7.7 fusion.46
  242.3 6.6 fusion.44
  248.9 96.3 %reduce-scatter.8.cloned.1.call-done = f32[2,128,2,768]{3,1,0,2:T(8,128)} async-done(((f32[2,1024,2,768]{3,1,0,2:T(8,128)}), f32[2,128,2,768]{3,1,0,2:T(8,128)}) %reduce-scatter.8.cloned.1.call-update) | async-done | bytes 1572880 | tf_op jit(solution)/shard_map/reduce_scatter | solution.py:191
  353.6 28.3 %reduce-scatter.16.cloned.1.call-done = f32[96,768]{1,0:T(8,128)} async-done(((f32[768,768]{1,0:T(8,128)}), f32[96,768]{1,0:T(8,128)}) %reduce-scatter.16.cloned.1.call-update) | async-done | bytes 294928 | tf_op jit(solution)/shard_map/reduce_scatter | solution.py:220
  381.9 37.7 %reduce-scatter.10.cloned.1.call-done = f32[96,768]{1,0:T(8,128)} async-done(((f32[768,768]{1,0:T(8,128)}), f32[96,768]{1,0:T(8,128)}) %reduce-scatter.10.cloned.1.call-update) | async-done | bytes 294928 | tf_op jit(solution)/shard_map/reduce_scatter | solution.py:217
  419.6 101.0 %reduce-scatter.20.cloned.1.call-done = f32[384,768]{1,0:T(8,128)} async-done(((f32[3072,768]{1,0:T(8,128)}), f32[384,768]{1,0:T(8,128)}) %reduce-scatter.20.cloned.1.call-update) | async-done | bytes 1179664 | tf_op jit(solution)/shard_map/reduce_scatter | solution.py:223
  520.6 100.2 %reduce-scatter.18.cloned.1.call-done = f32[96,3072]{1,0:T(8,128)} async-done(((f32[768,3072]{1,0:T(8,128)}), f32[96,3072]{1,0:T(8,128)}) %reduce-scatter.18.cloned.1.call-update) | async-done | bytes 1179664 | tf_op jit(solution)/shard_map/reduce_scatter | solution.py:222
  620.8 36.8 %reduce-scatter.14.cloned.1.call-done = f32[96,768]{1,0:T(8,128)} async-done(((f32[768,768]{1,0:T(8,128)}), f32[96,768]{1,0:T(8,128)}) %reduce-scatter.14.cloned.1.call-update) | async-done | bytes 294928 | tf_op jit(solution)/shard_map/reduce_scatter | solution.py:219
  657.6 37.9 %reduce-scatter.12.cloned.1.call-done = f32[96,768]{1,0:T(8,128)} async-done(((f32[768,768]{1,0:T(8,128)}), f32[96,768]{1,0:T(8,128)}) %reduce-scatter.12.cloned.1.call-update) | async-done | bytes 294928 | tf_op jit(solution)/shard_map/reduce_scatter | solution.py:218
  697.5 9.1 %copy.59 = f32[12,128,1024]{1,0,2:T(8,128)} copy(f32[12,128,1024]{2,1,0:T(8,128)} %get-tuple-element.90) | data formatting | bytes 12582912 | tf_op jit(solution)/shard_map/while/body/eval_jaxpr/reduce_sum | solution.py:185
  708.7 11.2 %convolution_bitcast_fusion.1 = f32[32,12]{1,0:T(8,128)S(1)} fusion(f32[12,128,1024]{1,0,2:T(8,128)} %copy.59, s32[128,1024]{0,1:T(8,128)} %copy-done.15), kind=kOutput, calls=%fused_computation.35 | convolution fusion | flops 608174080 | bytes 6817280 | tf_op jit(solution)/shard_map/hqk,nqk->nh/dot_general | solution.py:203
  727.6 26.1 %all-reduce.3 = (f32[768]{0:T(1024)S(1)}, f32[768]{0:T(1024)S(1)}, f32[32,12]{1,0:T(8,128)S(1)}) all-reduce(f32[768]{0:T(1024)S(1)} %get-tuple-element.64, f32[768]{0:T(1024)S(1)} %copy-done.38, f32[32,12]{1,0:T(8,128)S(1)} %convolution_bitcast_fusion.1), channel_id=3, replica_groups=mesh['dp'=4,'blk'=8] {'blk'}, use_global_device_ids=true, to_apply=%region_9.10.clone | all-reduce | flops 1920 | bytes 15360
  753.8 7.6 all-reduce.4
  763.5 32.2 %all-reduce.8.cloned.1.call-done = (f32[96,768]{1,0:T(8,128)}, f32[96,768]{1,0:T(8,128)}, f32[96,768]{1,0:T(8,128)}, f32[96,768]{1,0:T(8,128)}, f32[96,3072]{1,0:T(8,128)}, /*index=5*/f32[384,768]{1,0:T(8,128)}) async-done(((f32[96,768]{1,0:T(8,128)}, f32[96,768]{1,0:T(8,128)}, f32[96,768]{1,0:T(8,128)}, f32[96,768]{1,0:T(8,128)}, f32[96,3072]{1,0:T(8,128)}, /*index=5*/f32[384,768]{1,0:T(8,128)}), ...) | async-done | bytes 3538960 | tf_op jit(solution)/shard_map/psum | solution.py:226
  (182 shorter events, 99.7 us)
Async XLA Ops:
  7.2 7.7 copy-start.17
  7.2 107.4 %all-gather.5.cloned.1.call-start = ((), (), s32[]{:S(2)}) async-start(), calls=%async_computation.8 | async-start | bytes 3538944 | tf_op jit(solution)/shard_map/all_gather | solution.py:103
  13.5 120.6 %all-gather.3.cloned.1.call-start = ((), (), s32[]{:S(2)}) async-start(), calls=%async_computation.7 | async-start | bytes 3538944 | tf_op jit(solution)/shard_map/all_gather | solution.py:104
  14.8 330.4 %reduce-scatter.8.cloned.1.call-start = ((), (), s32[]{:S(2)}) async-start(), calls=%async_computation.9 | async-start | bytes 14155776 | tf_op jit(solution)/shard_map/reduce_scatter | solution.py:191
  15.7 103.6 %copy-start.12 = (bf16[2,128,12,64]{1,0,3,2:T(2,128)(2,1)}, bf16[2,128,12,64]{1,0,3,2:T(2,128)(2,1)S(1)}, u32[]{:S(2)}) copy-start(bf16[2,128,12,64]{1,0,3,2:T(2,128)(2,1)S(1)} %squeeze.40) | copy-start | bytes 1179652
  18.6 74.4 %copy-start.35 = (bf16[32,12]{0,1:T(8,128)(2,1)S(1)}, bf16[32,12]{0,1:T(8,128)(2,1)}, u32[]{:S(2)}) copy-start(bf16[32,12]{0,1:T(8,128)(2,1)} %param.22) | copy-start | bytes 2308
  138.8 7.2 slice-start.4
  138.8 7.2 slice-start.5
  146.0 7.3 copy-start.8
  154.4 11.8 %slice-start.2 = ((s8[6291456]{0:T(1024)(128)(4,1)}), s8[2097152]{0:T(1024)(128)(4,1)S(1)}, s32[]{:S(2)}) async-start(s8[6291456]{0:T(1024)(128)(4,1)} %bitcast.104), calls=%async_computation.19 | async-start | bytes 4194304
  183.9 14.8 %copy-start.13 = (bf16[2,128,12,64]{1,0,3,2:T(2,128)(2,1)S(1)}, bf16[2,128,12,64]{1,0,3,2:T(2,128)(2,1)}, u32[]{:S(2)}) copy-start(bf16[2,128,12,64]{1,0,3,2:T(2,128)(2,1)} %copy-done.12) | copy-start | bytes 1179652
  220.3 161.6 %reduce-scatter.16.cloned.1.call-start = ((), (), s32[]{:S(2)}) async-start(), calls=%async_computation.13 | async-start | bytes 2654208 | tf_op jit(solution)/shard_map/reduce_scatter | solution.py:220
  223.4 196.2 %reduce-scatter.10.cloned.1.call-start = ((), (), s32[]{:S(2)}) async-start(), calls=%async_computation.10 | async-start | bytes 2654208 | tf_op jit(solution)/shard_map/reduce_scatter | solution.py:217
  231.4 9.7 %copy-start.18 = (bf16[2,128,12,64]{1,0,3,2:T(2,128)(2,1)}, bf16[2,128,12,64]{1,0,3,2:T(2,128)(2,1)S(1)}, u32[]{:S(2)}) copy-start(bf16[2,128,12,64]{1,0,3,2:T(2,128)(2,1)S(1)} %copy.54) | copy-start | bytes 1179652
  233.4 287.2 %reduce-scatter.20.cloned.1.call-start = ((), (), s32[]{:S(2)}) async-start(), calls=%async_computation.15 | async-start | bytes 10616832 | tf_op jit(solution)/shard_map/reduce_scatter | solution.py:223
  241.2 379.7 %reduce-scatter.18.cloned.1.call-start = ((), (), s32[]{:S(2)}) async-start(), calls=%async_computation.14 | async-start | bytes 10616832 | tf_op jit(solution)/shard_map/reduce_scatter | solution.py:222
  248.9 408.8 %reduce-scatter.14.cloned.1.call-start = ((), (), s32[]{:S(2)}) async-start(), calls=%async_computation.12 | async-start | bytes 2654208 | tf_op jit(solution)/shard_map/reduce_scatter | solution.py:219
  350.2 345.3 %reduce-scatter.12.cloned.1.call-start = ((), (), s32[]{:S(2)}) async-start(), calls=%async_computation.11 | async-start | bytes 2654208 | tf_op jit(solution)/shard_map/reduce_scatter | solution.py:218
  353.2 342.3 %copy-start.40 = (u32[32]{0:T(128)S(1)}, u32[32]{0:T(128)}, u32[]{:S(2)}) copy-start(u32[32]{0:T(128)} %constant.99) | copy-start | bytes 388
  353.3 442.4 %all-reduce.8.cloned.1.call-start = ((), (), s32[]{:S(2)}) async-start(), calls=%async_computation.16 | async-start | bytes 7077888 | tf_op jit(solution)/shard_map/psum | solution.py:226
  697.4 9.1 %copy-start.19 = (bf16[2,128,12,64]{1,0,3,2:T(2,128)(2,1)S(1)}, bf16[2,128,12,64]{1,0,3,2:T(2,128)(2,1)}, u32[]{:S(2)}) copy-start(bf16[2,128,12,64]{1,0,3,2:T(2,128)(2,1)} %copy-done.18) | copy-start | bytes 1179652
  708.7 11.3 %copy-start.5 = (f32[256,3072]{1,0:T(8,128)S(1)}, f32[256,3072]{1,0:T(8,128)}, u32[]{:S(2)}) copy-start(f32[256,3072]{1,0:T(8,128)} %copy-done.4) | copy-start | bytes 9437188
  795.7 6.9 copy-start.30
  795.7 7.9 copy-start.29
  (35 other events, 136.1 us)
Sparse Core Ops, SparseCore 0:
  13.6 39.9 all-gather.4
  55.8 37.1 all-gather.2
  220.4 124.7 reduce-scatter.7
  347.4 34.4 reduce-scatter.15
  384.1 35.5 reduce-scatter.9
  421.8 98.8 reduce-scatter.19
  522.9 97.8 reduce-scatter.17
  623.2 34.4 reduce-scatter.13
  660.0 35.5 reduce-scatter.11
  699.2 96.4 all-reduce.7
where the time goes:
time: 823 us; the launch traced here: 812 us
  waiting for transfers between devices  471 us (57%)
  local copies, waits for them, and re-layouts  135 us (16%)
  matrix products  98.3 us (12%)
  blocking collectives  46.6 us (6%)
  other arithmetic  44.1 us (5%)
  between operations  16.6 us (2%)
    reduce_scatter x1, waiting for transfers between devices, on_device(): lax.psum_scatter(grads[7], 'blk', scatter_dimension=0, tiled=True)  101 us
    reduce_scatter x1, waiting for transfers between devices, on_device(): lax.psum_scatter(grads[6], 'blk', scatter_dimension=0, tiled=True)  100 us
    reduce_scatter x1, waiting for transfers between devices, on_device(): lax.psum_scatter(paired, 'blk', scatter_dimension=1, tiled=True)  96.3 us
    eq x1, local copies, waits for them, and re-layouts, on_device(): bucket_of(offsets)[None]  74.4 us
    reduce_scatter x1, waiting for transfers between devices, on_device(): lax.psum_scatter(grads[2], 'blk', scatter_dimension=0, tiled=True)  37.9 us
    reduce_scatter x1, waiting for transfers between devices, on_device(): lax.psum_scatter(grads[1], 'blk', scatter_dimension=0, tiled=True)  37.7 us
    reduce_scatter x1, waiting for transfers between devices, on_device(): lax.psum_scatter(grads[3], 'blk', scatter_dimension=0, tiled=True)  36.8 us
    psum x1, waiting for transfers between devices, on_device(): lax.psum((pieces[0], pieces[1], pieces[2], pieces[3], pieces[4], pieces[5...  32.2 us
  transfers between devices with their start and end apart: 10, of which 8 were waited for; matrix products, arithmetic and copies ran while one was open for 21% of the time, Pallas kernels for 0%

commit v1 on v0

--- a/solution.py
+++ b/solution.py
@@ -1,8 +1,11 @@
+import functools
 import math
 
 import jax
 import jax.numpy as jnp
 from jax import lax
+from jax.experimental import pallas as pl
+from jax.experimental.pallas import tpu as pltpu
 from jax.sharding import PartitionSpec as P
 
 EPS = 1e-06
@@ -252,6 +255,616 @@
     )
 
 
+BF = jnp.bfloat16
+F32 = jnp.float32
+MESH = pl.DeviceIdType.MESH
+VLIMIT = 60 * 1024 * 1024
+TILE = 128
+REACH = 511
+
+
+def mm(a, b):
+    return lax.dot_general(a, b, (((1,), (0,)), ((), ())), preferred_element_type=F32)
+
+
+def mm_nt(a, b):
+    return lax.dot_general(a, b, (((1,), (1,)), ((), ())), preferred_element_type=F32)
+
+
+def mm_tn(a, b):
+    return lax.dot_general(a, b, (((0,), (0,)), ((), ())), preferred_element_type=F32)
+
+
+def iota(shape, dim):
+    return lax.broadcasted_iota(jnp.int32, shape, dim)
+
+
+def spot():
+    blk = lax.axis_index("blk")
+    return lax.axis_index("dp"), blk // 2, blk % 2
+
+
+def gather_kernel(nz, tok, dy, seg, xrow, dyrow, segall, zero, segbuf, s_sem, r_sem, l_sem):
+    dp, z, c = spot()
+    blk = 2 * z + c
+    block = tok.shape[1]
+    nb = 2 * nz
+    barrier = pltpu.get_barrier_semaphore()
+    for k in range(1, nb):
+        pl.semaphore_signal(
+            barrier, inc=1, device_id=(dp, lax.rem(blk + k, nb)), device_id_type=MESH
+        )
+    pl.semaphore_wait(barrier, nb - 1)
+
+    def copy(src, dst, send, recv, zz, cc):
+        return pltpu.make_async_remote_copy(
+            src, dst, s_sem.at[send], r_sem.at[recv], device_id=(dp, 2 * zz + cc), device_id_type=MESH
+        )
+
+    mine = xrow.at[blk]
+    for hop, dz in ((0, 1), (1, -1)):
+
+        @pl.when((z + dz >= 0) & (z + dz < nz))
+        def _():
+            copy(tok.at[1 - c], mine, 2 * hop, blk, z + dz, 1 - c).start()
+            copy(tok.at[c], mine, 2 * hop + 1, blk, z + dz, c).start()
+
+    copy(tok.at[1 - c], mine, 4, blk, z, 1 - c).start()
+    copy(dy.at[1 - c], dyrow.at[c], 5, nb, z, 1 - c).start()
+    segbuf[...] = jnp.zeros_like(segbuf)
+    segbuf[0:2, :] = seg[...]
+    for k in range(1, nb):
+        to = lax.rem(blk + k, nb)
+        pltpu.make_async_remote_copy(
+            segbuf,
+            segall.at[blk],
+            s_sem.at[10 + k],
+            r_sem.at[nb + 1 + blk],
+            device_id=(dp, to),
+            device_id_type=MESH,
+        ).start()
+    segall[blk] = segbuf[...]
+    own = pltpu.make_async_copy(tok.at[c], mine, l_sem.at[0])
+    own.start()
+    own_dy = pltpu.make_async_copy(dy.at[c], dyrow.at[c], l_sem.at[1])
+    own_dy.start()
+
+    reach = -(-REACH // (2 * block))
+    for b in range(nb):
+
+        @pl.when(jnp.abs(b // 2 - z) > reach)
+        def _():
+            xrow[b] = jnp.zeros(xrow.shape[1:], xrow.dtype)
+
+    def arrived(b):
+        copy(tok.at[0], xrow.at[b], 0, b, z, 1 - c).wait_recv()
+
+    for far in range(1, reach + 1):
+        for way, dz in ((0, 1), (1, -1)):
+            src = z - dz * far
+
+            @pl.when((src >= 0) & (src < nz))
+            def _():
+                for h in range(2):
+                    arrived(2 * src + h)
+                    if far < reach:
+
+                        @pl.when((z + dz >= 0) & (z + dz < nz))
+                        def _():
+                            copy(
+                                xrow.at[2 * src + h],
+                                xrow.at[2 * src + h],
+                                6 + 2 * way + h,
+                                2 * src + h,
+                                z + dz,
+                                c,
+                            ).start()
+
+    arrived(2 * z + 1 - c)
+    copy(dy.at[0], dyrow.at[1 - c], 0, nb, z, 1 - c).wait_recv()
+    for k in range(1, nb):
+        frm = lax.rem(blk + nb - k, nb)
+        copy(segbuf, segall.at[frm], 0, nb + 1 + frm, z, 1 - c).wait_recv()
+    own.wait()
+    own_dy.wait()
+    for hop, dz in ((0, 1), (1, -1)):
+
+        @pl.when((z + dz >= 0) & (z + dz < nz))
+        def _():
+            copy(tok.at[0], mine, 2 * hop, blk, z, 1 - c).wait_send()
+            copy(tok.at[0], mine, 2 * hop + 1, blk, z, 1 - c).wait_send()
+
+        for far in range(1, reach):
+            src = z - dz * far
+
+            @pl.when((src >= 0) & (src < nz) & (z + dz >= 0) & (z + dz < nz))
+            def _():
+                for h in range(2):
+                    copy(tok.at[0], mine, 6 + 2 * hop + h, blk, z, 1 - c).wait_send()
+
+    copy(tok.at[0], mine, 4, blk, z, 1 - c).wait_send()
+    copy(dy.at[0], dyrow.at[0], 5, nb, z, 1 - c).wait_send()
+    for k in range(1, nb):
+        copy(segbuf, segall.at[0], 10 + k, nb + 1, z, 1 - c).wait_send()
+
+
+def gather(nz, tok, dy, seg):
+    _, block, width = tok.shape
+    nb = 2 * nz
+    vm = pl.BlockSpec(memory_space=pltpu.VMEM)
+    return pl.pallas_call(
+        functools.partial(gather_kernel, nz),
+        out_shape=(
+            jax.ShapeDtypeStruct((nb, block, width), BF),
+            jax.ShapeDtypeStruct((2, block, width), BF),
+            jax.ShapeDtypeStruct((nb, 8, block), jnp.int32),
+        ),
+        in_specs=[vm] * 3,
+        out_specs=(vm, vm, vm),
+        scratch_shapes=[
+            pltpu.VMEM((8, 128), F32),
+            pltpu.VMEM((8, block), jnp.int32),
+            pltpu.SemaphoreType.DMA((10 + nb,)),
+            pltpu.SemaphoreType.DMA((2 * nb + 2,)),
+            pltpu.SemaphoreType.DMA((2,)),
+        ],
+        compiler_params=pltpu.CompilerParams(
+            collective_id=1, has_side_effects=True, vmem_limit_bytes=VLIMIT
+        ),
+    )(tok, dy, seg)
+
+
+def norm_rows(x, gain):
+    x = x.astype(F32)
+    scale = lax.rsqrt(jnp.mean(x * x, axis=-1, keepdims=True) + EPS)
+    normed = x * scale
+    return normed, scale, (normed * gain).astype(BF)
+
+
+def prepare_bias(table_ref, near, heads):
+    buckets = table_ref.shape[0]
+    for d in range(3):
+        lane = iota((buckets, 2 * TILE), 1)
+        back = jnp.where(lane < TILE, lane, lane - 2 * TILE)
+        hot = (bucket_of((d - 1) * TILE - back) == iota((buckets, 2 * TILE), 0)).astype(BF)
+        strip = mm_tn(table_ref[...], hot)
+        for h in range(heads):
+            row = jnp.broadcast_to(strip[h : h + 1, :], (TILE, 2 * TILE))
+            near[h, d] = pltpu.roll(row, 0, 1, stride=1, stride_axis=0)[:, :TILE]
+
+
+def prepare_masks(segall, kaug, qseg, qright, qleft, z, c, tq):
+    nkb = kaug.shape[0] // TILE
+    for b in range(nkb):
+        row = segall[b, pl.ds(c, 1), :]
+        r = iota((TILE, TILE), 0)
+        hot = jnp.where((r == row) | (r == 8 + b), 1.0, 0.0).astype(F32)
+        kaug[b * TILE : (b + 1) * TILE, :] = hot.T.astype(BF)
+    for i in range(tq // TILE):
+        qb = (tq // TILE) * z + i
+        row = segall[qb, pl.ds(c, 1), :]
+        r = iota((TILE, TILE), 0)
+        lost = jnp.where((r < 8) & (r != row), NEG, 0.0).astype(F32)
+        qseg[i * TILE : (i + 1) * TILE, :] = lost.T
+        col = iota((TILE, TILE), 1) - 8
+        ok = (col >= 0) & (col < nkb)
+        qright[i * TILE : (i + 1) * TILE, :] = jnp.where(ok & (col >= qb + 2), 1.0, 0.0)
+        qleft[i * TILE : (i + 1) * TILE, :] = jnp.where(ok & (col <= qb - 2), 1.0, 0.0)
+
+
+def stacked(ref, cols, dst, tq):
+    part = ref[:, cols].astype(F32)
+    low = iota((tq, TILE), 1) < TILE // 2
+    dst[0:tq, 0:TILE] = jnp.where(low, part, 0.0).astype(BF)
+    dst[tq : 2 * tq, 0:TILE] = jnp.where(low, 0.0, part).astype(BF)
+
+
+def attn_forward_pair(p, z, q, k, v, kaug, qseg, qright, qleft, near, ts, probs, att, qa, s):
+    tq = q.shape[0]
+    length = k.shape[0]
+    nkb = length // TILE
+    cols = pl.ds(pl.multiple_of(p * TILE, TILE), TILE)
+    stacked(q, cols, qa, tq)
+    for hh in range(2):
+        far = ts[31, 2 * p + hh] * qright[...] + ts[15, 2 * p + hh] * qleft[...] + qseg[...]
+        qa[hh * tq : (hh + 1) * tq, TILE:] = far.astype(BF)
+
+    def score(rb, carry):
+        rows = pl.ds(pl.multiple_of(rb * TILE, TILE), TILE)
+        left = jnp.concatenate([k[rows, cols], kaug[rows, :]], axis=1)
+        s[pl.ds(pl.multiple_of((rb + 1) * TILE, TILE), TILE), :] = mm_nt(left, qa[...])
+        return carry
+
+    lax.fori_loop(0, nkb, score, 0)
+    for i in range(tq // TILE):
+        for d in range(3):
+            row = ((tq // TILE) * z + i + d) * TILE
+            rows = pl.ds(pl.multiple_of(row, TILE), TILE)
+            for hh in range(2):
+                at = hh * tq + i * TILE
+                s[rows, at : at + TILE] = s[rows, at : at + TILE] + near[2 * p + hh, d]
+
+    def top(rb, best):
+        rows = pl.ds(pl.multiple_of((rb + 1) * TILE, TILE), TILE)
+        return jnp.maximum(best, jnp.max(s[rows, :].reshape(TILE // 8, 8, 2 * tq), axis=0))
+
+    best = lax.fori_loop(0, nkb, top, jnp.full((8, 2 * tq), -3e38, F32))
+    best = jnp.max(best, axis=0, keepdims=True)
+
+    def expo(rb, total):
+        rows = pl.ds(pl.multiple_of((rb + 1) * TILE, TILE), TILE)
+        e = jnp.exp(s[rows, :] - best)
+        s[rows, :] = e
+        return total + jnp.sum(e.reshape(TILE // 8, 8, 2 * tq), axis=0)
+
+    total = lax.fori_loop(0, nkb, expo, jnp.zeros((8, 2 * tq), F32))
+    inverse = 1.0 / jnp.sum(total, axis=0, keepdims=True)
+
+    def finish(rb, carry):
+        rows = pl.ds(pl.multiple_of(rb * TILE, TILE), TILE)
+        at = pl.ds(pl.multiple_of((rb + 1) * TILE, TILE), TILE)
+        probs[p, rows, :] = (s[at, :] * inverse).astype(BF)
+        return carry
+
+    lax.fori_loop(0, nkb, finish, 0)
+    mixed = mm_tn(v[:, cols], probs[p])
+    both = jnp.concatenate([mixed[: TILE // 2, :tq], mixed[TILE // 2 :, tq:]], axis=0)
+    att[:, cols] = both.T.astype(BF)
+
+
+def forward_kernel(
+    xrow, segall, gain, wq, wk, wv, table, ts, n1, k, v, q, probs, att,
+    kaug, qseg, qright, qleft, near, qa, s,
+):
+    _, z, c = spot()
+    nb, block, _ = xrow.shape
+    tq = 2 * block
+    g = gain[...].astype(F32)
+    prepare_bias(table, near, 2 * probs.shape[0])
+    prepare_masks(segall, kaug, qseg, qright, qleft, z, c, tq)
+    for b in range(nb // 2):
+        rows = slice(b * tq, (b + 1) * tq)
+        part = xrow[2 * b : 2 * b + 2].reshape(tq, xrow.shape[2])
+        n1[rows, :] = norm_rows(part, g)[2]
+        k[rows, :] = mm(n1[rows, :], wk[...]).astype(BF)
+        v[rows, :] = mm(n1[rows, :], wv[...]).astype(BF)
+    own = n1[pl.ds(pl.multiple_of(z * tq, tq), tq), :]
+    q[...] = mm(own, wq[...]).astype(BF)
+    s[0:TILE, :] = jnp.zeros((TILE, s.shape[1]), F32)
+    s[s.shape[0] - TILE :, :] = jnp.zeros((TILE, s.shape[1]), F32)
+
+    def pair(p, carry):
+        attn_forward_pair(p, z, q, k, v, kaug, qseg, qright, qleft, near, ts, probs, att, qa, s)
+        return carry
+
+    lax.fori_loop(0, probs.shape[0], pair, 0)
+
+
+def forward(xrow, segall, gain, wq, wk, wv, table):
+    nb, block, width = xrow.shape
+    length, tq = nb * block, 2 * block
+    inner = wq.shape[1]
+    heads = table.shape[1]
+    pairs = heads // 2
+    vm = pl.BlockSpec(memory_space=pltpu.VMEM)
+    sm = pl.BlockSpec(memory_space=pltpu.SMEM)
+    return pl.pallas_call(
+        forward_kernel,
+        out_shape=(
+            jax.ShapeDtypeStruct((length, width), BF),
+            jax.ShapeDtypeStruct((length, inner), BF),
+            jax.ShapeDtypeStruct((length, inner), BF),
+            jax.ShapeDtypeStruct((tq, inner), BF),
+            jax.ShapeDtypeStruct((pairs, length, 2 * tq), BF),
+            jax.ShapeDtypeStruct((tq, inner), BF),
+        ),
+        in_specs=[vm] * 7 + [sm],
+        out_specs=(vm,) * 6,
+        scratch_shapes=[
+            pltpu.VMEM((length, TILE), BF),
+            pltpu.VMEM((tq, TILE), F32),
+            pltpu.VMEM((tq, TILE), F32),
+            pltpu.VMEM((tq, TILE), F32),
+            pltpu.VMEM((heads, 3, TILE, TILE), F32),
+            pltpu.VMEM((2 * tq, 2 * TILE), BF),
+            pltpu.VMEM((length + 2 * TILE, 2 * tq), F32),
+        ],
+        compiler_params=pltpu.CompilerParams(vmem_limit_bytes=VLIMIT),
+    )(xrow, segall, gain, wq, wk, wv, table, table.astype(F32))
+
+
+def ffn_kernel(
+    xown, att, dy, gain, wout, win, wdown, out, dh, datt, pdown, pin, pout, gfin,
+    n2, act, slope,
+):
+    tq, width = att.shape[0], wout.shape[1]
+    inner = win.shape[1]
+    nb = pdown.shape[0]
+    wide = width
+    steps = inner // wide
+    g = gain[...].astype(F32)
+    h = xown[...].reshape(tq, width).astype(F32) + mm(att[...], wout[...])
+    normed, scale, low = norm_rows(h, g)
+    n2[...] = low
+    d = dy[...].reshape(tq, width)
+    total = h
+    for j in range(steps):
+        cols = slice(j * wide, (j + 1) * wide)
+        value, slant = gelu_both(mm(n2[...], win[:, cols]))
+        act[:, cols] = value.astype(BF)
+        slope[:, cols] = slant
+        total = total + mm(act[:, cols], wdown[cols, :])
+    out[...] = total.astype(BF).reshape(out.shape)
+    per = inner // nb
+    quarters = pdown.shape[1]
+    for j in range(steps):
+        cols = slice(j * wide, (j + 1) * wide)
+        grad = mm_tn(act[:, cols], d).astype(BF)
+        count = wide // per
+        pdown[j * count : (j + 1) * count] = grad.reshape(count, quarters, per // quarters, width)
+    dn2 = jnp.zeros((tq, width), F32)
+    for j in range(steps):
+        cols = slice(j * wide, (j + 1) * wide)
+        dpre = (mm_nt(d, wdown[cols, :]) * slope[:, cols]).astype(BF)
+        pin[:, j] = mm_tn(n2[...], dpre).astype(BF).reshape(nb, width // nb, wide)
+        dn2 = dn2 + mm_nt(dpre, win[:, cols])
+    back, gain_grad = rms_backward(dn2, normed, scale, g)
+    gfin[...] = gain_grad[None]
+    dhid = d.astype(F32) + back
+    dh[...] = dhid
+    dhl = dhid.astype(BF)
+    pout[...] = mm_tn(att[...], dhl).astype(BF).reshape(nb, width // nb, width)
+    datt[...] = mm_nt(dhl, wout[...]).astype(BF)
+
+
+def ffn(xown, att, dy, gain, wout, win, wdown, nb, quarters):
+    tq, width = att.shape[0], wout.shape[1]
+    inner = win.shape[1]
+    vm = pl.BlockSpec(memory_space=pltpu.VMEM)
+    return pl.pallas_call(
+        ffn_kernel,
+        out_shape=(
+            jax.ShapeDtypeStruct((2, tq // 2, width), BF),
+            jax.ShapeDtypeStruct((tq, width), F32),
+            jax.ShapeDtypeStruct((tq, att.shape[1]), BF),
+            jax.ShapeDtypeStruct((nb, quarters, inner // nb // quarters, width), BF),
+            jax.ShapeDtypeStruct((nb, quarters, width // nb, inner // quarters), BF),
+            jax.ShapeDtypeStruct((nb, width // nb, width), BF),
+            jax.ShapeDtypeStruct((1, width), F32),
+        ),
+        in_specs=[vm] * 7,
+        out_specs=(vm,) * 7,
+        scratch_shapes=[
+            pltpu.VMEM((tq, width), BF),
+            pltpu.VMEM((tq, inner), BF),
+            pltpu.VMEM((tq, inner), F32),
+        ],
+        compiler_params=pltpu.CompilerParams(vmem_limit_bytes=VLIMIT),
+    )(xown, att, dy, gain, wout, win, wdown)
+
+
+def attn_backward_pair(p, z, q, k, v, kaug, datt, probs, dk, dv, dq, near, far, qm, dm, dprob, ds):
+    tq = q.shape[0]
+    length = k.shape[0]
+    nkb = length // TILE
+    cols = pl.ds(pl.multiple_of(p * TILE, TILE), TILE)
+    stacked(q, cols, qm, tq)
+    stacked(datt, cols, dm, tq)
+
+    def first(rb, total):
+        rows = pl.ds(pl.multiple_of(rb * TILE, TILE), TILE)
+        part = mm_nt(v[rows, cols], dm[...])
+        dprob[rows, :] = part
+        mixed = part * probs[p, rows, :].astype(F32)
+        dv[rows, cols] = mm(probs[p, rows, :], dm[...]).astype(BF)
+        return total + jnp.sum(mixed.reshape(TILE // 8, 8, 2 * tq), axis=0)
+
+    total = lax.fori_loop(0, nkb, first, jnp.zeros((8, 2 * tq), F32))
+    center = jnp.sum(total, axis=0, keepdims=True)
+
+    def second(rb, carry):
+        rows = pl.ds(pl.multiple_of(rb * TILE, TILE), TILE)
+        at = pl.ds(pl.multiple_of((rb + 1) * TILE, TILE), TILE)
+        part = (probs[p, rows, :].astype(F32) * (dprob[rows, :] - center)).astype(BF)
+        ds[at, :] = part
+        dk[rows, cols] = mm(part, qm[...]).astype(BF)
+        return carry
+
+    lax.fori_loop(0, nkb, second, 0)
+    left = jnp.concatenate([k[:, cols], kaug[...]], axis=1)
+    back = mm_tn(left, ds[TILE : TILE + length, :])
+    both = jnp.concatenate([back[: TILE // 2, :tq], back[TILE // 2 : TILE, tq:]], axis=0)
+    dq[:, cols] = both.T.astype(BF)
+    sums = back[TILE + 8 : TILE + 8 + nkb, :]
+    kb = iota((nkb, 2 * tq), 0)
+    lane = iota((nkb, 2 * tq), 1)
+    qb = (tq // TILE) * z + (lane % tq) // TILE
+    far[0, pl.ds(p, 1), :] = jnp.sum(jnp.where(kb >= qb + 2, sums, 0.0), axis=0, keepdims=True)
+    far[1, pl.ds(p, 1), :] = jnp.sum(jnp.where(kb <= qb - 2, sums, 0.0), axis=0, keepdims=True)
+    for hh in range(2):
+        for d in range(3):
+            acc = jnp.zeros((TILE, TILE), F32)
+            for i in range(tq // TILE):
+                row = ((tq // TILE) * z + i + d) * TILE
+                at = hh * tq + i * TILE
+                acc = acc + ds[pl.ds(pl.multiple_of(row, TILE), TILE), at : at + TILE].astype(F32)
+            near[2 * p + hh, d] = acc
+
+
+def table_sums(near, far, rows, small, first_row, tq):
+    heads = near.shape[0]
+    rows[...] = jnp.zeros_like(rows)
+    for d in range(3):
+        offset = (d - 1) * TILE + iota((TILE, TILE), 0) - iota((TILE, TILE), 1)
+        bucket = bucket_of(offset)
+        for b in range(32):
+            if (d == 0 and b >= 16) or (d == 2 and b < 16):
+                continue
+            hit = bucket == b
+
+            def one(h, carry):
+                part = jnp.where(hit, near[h, d], 0.0)
+                part = jnp.sum(part.reshape(TILE // 8, 8, TILE), axis=0)
+                rows[pl.ds(h, 1), b, :] = rows[pl.ds(h, 1), b, :] + jnp.sum(part, axis=0, keepdims=True)
+                return carry
+
+            lax.fori_loop(0, heads, one, 0)
+    for h in range(heads):
+        p, hh = h // 2, h % 2
+        for side, b in ((0, 31), (1, 15)):
+            line = far[side, p : p + 1, hh * tq : (hh + 1) * tq]
+            for i in range(tq // TILE):
+                rows[h, b : b + 1, :] = rows[h, b : b + 1, :] + line[:, i * TILE : (i + 1) * TILE]
+    for part in range(heads * 32 // TILE):
+        per = TILE // 32
+        square = rows[part * per : (part + 1) * per].reshape(TILE, TILE)
+        small[first_row + part : first_row + part + 1, :] = jnp.sum(square.T, axis=0, keepdims=True)
+
+
+def backward_kernel(
+    xrow, segall, gain, wq, wk, wv, n1, q, k, v, probs, datt, gfin, dpart, dqpart, pqkv, small,
+    kaug, dk, dv, dq, near, far, qm, dm, dprob, ds, rows,
+):
+    _, z, c = spot()
+    tq = q.shape[0]
+    length = k.shape[0]
+    width = n1.shape[1]
+    nkb = length // TILE
+    nb = pqkv.shape[0]
+    for b in range(nkb):
+        lane = iota((TILE, TILE), 1)
+        kaug[b * TILE : (b + 1) * TILE, :] = jnp.where(lane == 8 + b, 1.0, 0.0).astype(BF)
+    ds[0:TILE, :] = jnp.zeros((TILE, ds.shape[1]), BF)
+    ds[ds.shape[0] - TILE :, :] = jnp.zeros((TILE, ds.shape[1]), BF)
+
+    def pair(p, carry):
+        attn_backward_pair(
+            p, z, q, k, v, kaug, datt, probs, dk, dv, dq, near, far, qm, dm, dprob, ds
+        )
+        return carry
+
+    lax.fori_loop(0, probs.shape[0], pair, 0)
+    g = gain[...].astype(F32)
+    for i, (left, right) in enumerate(
+        ((n1[pl.ds(pl.multiple_of(z * tq, tq), tq), :], dq), (n1[...], dk), (n1[...], dv))
+    ):
+        pqkv[:, i] = mm_tn(left, right[...]).astype(BF).reshape(nb, width // nb, right.shape[1])
+    gain_sum = jnp.zeros((1, width), F32)
+    for b in range(length // tq):
+        rows_b = slice(b * tq, (b + 1) * tq)
+        part = mm_nt(dk[rows_b, :], wk[...]) + mm_nt(dv[rows_b, :], wv[...])
+        dpart[b] = part.astype(BF)
+        normed = norm_rows(xrow[2 * b : 2 * b + 2].reshape(tq, width), g)[0]
+        gain_sum = gain_sum + jnp.sum(part * normed, axis=0, keepdims=True)
+
+        @pl.when(b == z)
+        def _():
+            dqpart[...] = part
+
+    own = mm_nt(dq[...], wq[...])
+    dqpart[...] = dqpart[...] + own
+    normed = norm_rows(xrow[pl.ds(2 * z, 2)].reshape(tq, width), g)[0]
+    gain_sum = gain_sum + jnp.sum(own * normed, axis=0, keepdims=True)
+    small[...] = jnp.zeros_like(small)
+    lines = width // TILE
+    for i in range(lines):
+        small[i : i + 1, :] = gain_sum[:, i * TILE : (i + 1) * TILE]
+        small[lines + i : lines + i + 1, :] = gfin[:, i * TILE : (i + 1) * TILE]
+    table_sums(near, far, rows, small, 2 * lines, tq)
+
+
+def backward(xrow, segall, gain, wq, wk, wv, n1, q, k, v, probs, datt, gfin):
+    nb, block, width = xrow.shape
+    length, tq = nb * block, 2 * block
+    inner = wq.shape[1]
+    pairs = probs.shape[0]
+    vm = pl.BlockSpec(memory_space=pltpu.VMEM)
+    return pl.pallas_call(
+        backward_kernel,
+        out_shape=(
+            jax.ShapeDtypeStruct((length // tq, tq, width), BF),
+            jax.ShapeDtypeStruct((tq, width), F32),
+            jax.ShapeDtypeStruct((nb, 3, width // nb, inner), BF),
+            jax.ShapeDtypeStruct((16, TILE), F32),
+        ),
+        in_specs=[vm] * 13,
+        out_specs=(vm,) * 4,
+        scratch_shapes=[
+            pltpu.VMEM((length, TILE), BF),
+            pltpu.VMEM((length, inner), BF),
+            pltpu.VMEM((length, inner), BF),
+            pltpu.VMEM((tq, inner), BF),
+            pltpu.VMEM((2 * pairs, 3, TILE, TILE), F32),
+            pltpu.VMEM((2, 8, 2 * tq), F32),
+            pltpu.VMEM((2 * tq, TILE), BF),
+            pltpu.VMEM((2 * tq, TILE), BF),
+            pltpu.VMEM((length, 2 * tq), F32),
+            pltpu.VMEM((length + 2 * TILE, 2 * tq), BF),
+            pltpu.VMEM((2 * pairs, 32, TILE), F32),
+        ],
+        compiler_params=pltpu.CompilerParams(vmem_limit_bytes=VLIMIT),
+    )(xrow, segall, gain, wq, wk, wv, n1, q, k, v, probs, datt, gfin)
+
+
+def fast_device(
+    nz, tokens, segment_ids, gain_attn, w_query, w_key, w_value, w_out, gain_ffn, w_in, w_down,
+    rel_table, cotangent,
+):
+    rows, block, width = tokens.shape
+    nb, quarters = 2 * nz, 4
+    tq = 2 * block
+    z, c = lax.axis_index("blk") // 2, lax.axis_index("blk") % 2
+    xrow, dyrow, segall = gather(nz, tokens, cotangent, segment_ids)
+    g1, g2 = gain_attn.reshape(1, width), gain_ffn.reshape(1, width)
+    n1, k, v, q, probs, att = forward(xrow, segall, g1, w_query, w_key, w_value, rel_table)
+    xown = lax.dynamic_slice_in_dim(xrow, 2 * z, 2, 0)
+    out, dh, datt, pdown, pin, pout, gfin = ffn(
+        xown, att, dyrow, g2, w_out, w_in, w_down, nb, quarters
+    )
+    dpart, dqpart, pqkv, small = backward(
+        xrow, segall, g1, w_query, w_key, w_value, n1, q, k, v, probs, datt, gfin
+    )
+    def scatter(part):
+        return lax.psum(lax.psum_scatter(part.astype(F32), "blk", tiled=True), "dp")[0]
+
+    gdown = scatter(pdown).reshape(-1, width)
+    gin = jnp.transpose(scatter(pin), (1, 0, 2)).reshape(width // nb, -1)
+    gqkv = scatter(pqkv)
+    gout = scatter(pout)
+    flat = lax.psum(small, ("dp", "blk")).reshape(-1)
+    b = lax.axis_index("blk")
+    share = width // nb
+    ga = lax.dynamic_slice_in_dim(flat[:width], b * share, share)
+    gf = lax.dynamic_slice_in_dim(flat[width : 2 * width], b * share, share)
+    heads = rel_table.shape[1]
+    gt = flat[2 * width : 2 * width + 32 * heads].reshape(heads, 32).T
+    gt = lax.dynamic_slice_in_dim(gt, b * (32 // nb), 32 // nb)
+    every = lax.all_gather(dpart, "blk", axis=0).reshape(nz, 2, nz, tq, width)
+    mine = every[:, c][:, z].astype(F32)
+    keep = (jnp.arange(nz) != z)[:, None, None]
+    dn1 = dqpart + jnp.sum(jnp.where(keep, mine, 0.0), axis=0)
+    x = xown.reshape(tq, width).astype(F32)
+    normed, scale, _ = rms_forward(x, gain_attn.astype(F32))
+    back, _ = rms_backward(dn1, normed, scale, gain_attn.astype(F32))
+    grad_tokens = (dh + back).astype(BF).reshape(2, block, width)
+
+    def home(own):
+        pairs = [(i, i ^ 1) for i in range(nb)]
+        other = lax.ppermute(lax.dynamic_index_in_dim(own, 1 - c, 0, False), "blk", pairs)
+        kept = lax.dynamic_index_in_dim(own, c, 0, False)
+        return jnp.where(c == 0, jnp.stack([kept, other]), jnp.stack([other, kept]))
+
+    return (
+        home(out), home(grad_tokens), ga, gqkv[0], gqkv[1], gqkv[2], gout, gf, gin, gdown, gt,
+    )
+
+
+def pick(mesh):
+    if mesh.shape["dp"] == 4 and mesh.shape["blk"] == 8:
+        return functools.partial(fast_device, mesh.shape["blk"] // 2)
+    return on_device
+
+
 def solution(mesh):
     placed = (
         P("dp", "blk", None),
@@ -268,7 +881,7 @@
         P("dp", "blk", None),
     )
     return jax.shard_map(
-        on_device,
+        pick(mesh),
         mesh=mesh,
         in_specs=placed,
         out_specs=(

time: 823 us -> 634 us (0.77); the launches traced: 812 us -> 632 us
  Pallas kernels: 0 us -> 128 us
  local copies, waits for them, and re-layouts: 135 us -> 17.6 us
  matrix products: 98.3 us -> 0 us
  waiting for transfers between devices: 471 us -> 401 us
  other arithmetic: 44.1 us -> 27.5 us
    reduce_scatter x7 -> x4, waiting for transfers between devices: 438 us -> 235 us  [scatter(): lax.psum_scatter(part.astype(F32), 'blk', tiled=True)]
    pallas_call x0 -> x4, Pallas kernels: none -> 128 us  [the longest x1 58.5 us: backward(): pl.pallas_call(backward_kernel, out_shape=(jax.ShapeDtypeStruct((length /...]
    dot_general x26 -> x0, matrix products: 98.3 us -> none  [the longest x6 23 us: outer_sum(): jnp.einsum('td,tf->df', left, right, preferred_element_type=jnp.float32)]
    all_gather x2 -> x1, waiting for transfers between devices: 0.02 us -> 75.9 us  [fast_device(): every = lax.all_gather(dpart, 'blk', axis=0).reshape(nz, 2, nz, tq, width)]
    eq x1 -> x0, local copies, waits for them, and re-layouts: 74.4 us -> none  [on_device(): bucket_of(offsets)[None]]
    psum x1, waiting for transfers between devices: 32.2 us -> 88.9 us  [scatter(): lax.psum(lax.psum_scatter(part.astype(F32), 'blk', tiled=True), 'dp')[0]]
    psum x1, blocking collectives: 7.58 us -> 40.3 us  [fast_device(): flat = lax.psum(small, ('dp', 'blk')).reshape(-1)]
    unnamed x1 -> x0, blocking collectives: 26.1 us -> none
  transfers between devices with their start and end apart: 10 -> 8, of which waited for: 8 -> 6; matrix products, arithmetic and copies ran while one was open for 21% -> 4% of each run, Pallas kernels for 0% -> 9%
where the time goes in v1:
time: 634 us; the launch traced here: 632 us
  waiting for transfers between devices  401 us (63%)
  Pallas kernels  128 us (20%)
  blocking collectives  40.3 us (6%)
  other arithmetic  27.5 us (4%)
  local copies, waits for them, and re-layouts  17.6 us (3%)
  between operations  14.2 us (2%)
    reduce_scatter x4, waiting for transfers between devices, scatter(): lax.psum_scatter(part.astype(F32), 'blk', tiled=True)  235 us
    psum x1, waiting for transfers between devices, scatter(): lax.psum(lax.psum_scatter(part.astype(F32), 'blk', tiled=True), 'dp')[0]  88.9 us
    all_gather x1, waiting for transfers between devices, fast_device(): every = lax.all_gather(dpart, 'blk', axis=0).reshape(nz, 2, nz, tq, width)  75.9 us
    pallas_call x1, Pallas kernels, backward(): pl.pallas_call(backward_kernel, out_shape=(jax.ShapeDtypeStruct((length /...  58.5 us
    psum x1, blocking collectives, fast_device(): flat = lax.psum(small, ('dp', 'blk')).reshape(-1)  40.3 us
    pallas_call x1, Pallas kernels, forward(): pl.pallas_call(forward_kernel, out_shape=(jax.ShapeDtypeStruct((length, w...  28.2 us
    pallas_call x1, Pallas kernels, gather(): pl.pallas_call(functools.partial(gather_kernel, nz), out_shape=(jax.Shape...  25.7 us
    convert_element_type x4, other arithmetic, scatter(): part.astype(F32)  21.6 us
  transfers between devices with their start and end apart: 8, of which 6 were waited for; matrix products, arithmetic and copies ran while one was open for 4% of the time, Pallas kernels for 9%

profile of v1, /device:TPU:3, one launch (start us, length us, event | category | flops | bytes accessed | tf_op | source)
XLA Modules:
  0.0 631.7 jit_solution(9948489678837790575)
XLA Ops:
  7.2 1.4 copy.35.ts
  8.6 1.4 copy.34.table
  10.0 1.3 reshape.84.gain
  11.2 1.3 reshape.85.gain
  12.5 25.7 %shard_map.203 = (bf16[8,128,768]{2,1,0:T(8,128)(2,1)}, bf16[2,128,768]{2,1,0:T(8,128)(2,1)}, s32[8,8,128]{2,1,0:T(8,128)}) custom-call(bf16[2,128,768]{2,1,0:T(8,128)(2,1)} %tok.1, bf16[2,128,768]{2,1,0:T(8,128)(2,1)} %dy.1, s32[2,128]{1,0:T(2,128)} %seg.1), custom_call_target="tpu_custom_call" | custom-call | tf_op jit(solution)/shard_map/pallas_call | solution.py:395
  38.2 1.8 multiply_reduce_fusion.1
  40.0 28.2 %shard_map.204 = (bf16[1024,768]{1,0:T(8,128)(2,1)}, bf16[1024,768]{1,0:T(8,128)(2,1)}, bf16[1024,768]{1,0:T(8,128)(2,1)}, bf16[256,768]{1,0:T(8,128)(2,1)}, bf1...) custom-call(bf16[8,128,768]{2,1,0:T(8,128)(2,1)} %get-tuple-element.31.xrow, s32[8,8,128]{2,1,0:T(8,128)} %get-tuple-element.32.segall, ...), custom_call_target="tpu_custom_call" | custom-call | tf_op jit(solution)/shard_map/pallas_call | solution.py:551
  68.2 15.7 %shard_map.205 = (bf16[2,128,768]{2,1,0:T(8,128)(2,1)}, f32[256,768]{1,0:T(8,128)}, bf16[256,768]{1,0:T(8,128)(2,1)}, bf16[8,4,96,768]{3,2,1,0:T(8,128)(2,1)}, b...) custom-call(bf16[2,128,768]{2,1,0:T(8,128)(2,1)} %get-tuple-element.56.xown, ...), custom_call_target="tpu_custom_call" | custom-call | tf_op jit(solution)/shard_map/pallas_call | solution.py:624
  83.9 7.1 %convert_element_type.46 = f32[8,4,96,768]{3,2,1,0:T(8,128)} convert(bf16[8,4,96,768]{3,2,1,0:T(8,128)(2,1)} %get-tuple-element.49) | non-fusion elementwise | flops 2359296 | bytes 14155776 | tf_op jit(solution)/shard_map/convert_element_type | solution.py:828
  92.2 1.6 convert_element_type.45
  93.9 58.5 %shard_map.206 = (bf16[4,256,768]{2,1,0:T(8,128)(2,1)}, f32[256,768]{1,0:T(8,128)}, bf16[8,3,96,768]{3,2,1,0:T(8,128)(2,1)}, f32[16,128]{1,0:T(8,128)}) custom-call(bf16[8,128,768]{2,1,0:T(8,128)(2,1)} %get-tuple-element.31.xrow, s32[8,8,128]{2,1,0:T(8,128)} %get-tuple-element.32.segall, bf16[1,768]{1,0:T(2,128)(2,1)} %reshape.84.gain, bf16[768,768]{1,0:T(8,128)(2,1)} %wq.3, ...), custom_call_target="tpu_custom_call" | custom-call | tf_op jit(solution)/shard_map/pallas_call | solution.py:782
  152.4 5.8 convert_element_type.44
  158.3 7.1 %convert_element_type.47 = f32[8,4,96,768]{3,2,1,0:T(8,128)} convert(bf16[8,4,96,768]{3,2,1,0:T(8,128)(2,1)} %get-tuple-element.50) | non-fusion elementwise | flops 2359296 | bytes 14155776 | tf_op jit(solution)/shard_map/convert_element_type | solution.py:828
  166.1 21.7 %reduce-scatter.9.cloned.1.call-done = f32[1,4,96,768]{3,2,1,0:T(8,128)} async-done(((f32[8,4,96,768]{3,2,1,0:T(8,128)}), f32[1,4,96,768]{3,2,1,0:T(8,128)}) %reduce-scatter.9.cloned.1.call-update) | async-done | bytes 1179664 | tf_op jit(solution)/shard_map/reduce_scatter | solution.py:828
  187.8 2.4 copy.39
  190.2 34.4 %reduce-scatter.7.cloned.1.call-done = f32[1,96,768]{2,1,0:T(8,128)} async-done(((f32[8,96,768]{2,1,0:T(8,128)}), f32[1,96,768]{2,1,0:T(8,128)}) %reduce-scatter.7.cloned.1.call-update) | async-done | bytes 294928 | tf_op jit(solution)/shard_map/reduce_scatter | solution.py:828
  224.6 79.0 %reduce-scatter.5.cloned.1.call-done = f32[1,3,96,768]{3,2,1,0:T(8,128)} async-done(((f32[8,3,96,768]{3,2,1,0:T(8,128)}), f32[1,3,96,768]{3,2,1,0:T(8,128)}) %reduce-scatter.5.cloned.1.call-update) | async-done | bytes 884752 | tf_op jit(solution)/shard_map/reduce_scatter | solution.py:828
  303.6 100.1 %reduce-scatter.11.cloned.1.call-done = f32[1,4,96,768]{3,2,1,0:T(8,128)} async-done(((f32[8,4,96,768]{3,2,1,0:T(8,128)}), f32[1,4,96,768]{3,2,1,0:T(8,128)}) %reduce-scatter.11.cloned.1.call-update) | async-done | bytes 1179664 | tf_op jit(solution)/shard_map/reduce_scatter | solution.py:828
  404.7 2.9 collective-permute-start
  407.6 40.3 %psum.35 = f32[16,128]{1,0:T(8,128)S(1)} all-reduce(f32[16,128]{1,0:T(8,128)S(1)} %copy-done.9), channel_id=1, replica_groups=mesh['dp'=4,'blk'=8] {'dp','blk'}, use_global_device_ids=true, to_apply=%region_3.4 | all-reduce | flops 2048 | bytes 16384 | tf_op jit(solution)/shard_map/psum | solution.py:834
  448.0 75.9 %all-gather.3.cloned.1.call-done = bf16[32,256,768]{2,1,0:T(8,128)(2,1)} async-done(((bf16[4,256,768]{2,1,0:T(8,128)(2,1)}), bf16[32,256,768]{2,1,0:T(8,128)(2,1)}) %all-gather.3.cloned.1.call-update) | async-done | bytes 12582928 | tf_op jit(solution)/shard_map/all_gather | solution.py:842
  523.8 1.9 fusion
  531.0 88.9 %all-reduce.3.cloned.1.call-done = (f32[1,3,96,768]{3,2,1,0:T(8,128)}, f32[96,768]{1,0:T(8,128)}, f32[96,3072]{1,0:T(8,128)}, f32[384,768]{1,0:T(8,128)}) async-done(((f32[1,3,96,768]{3,2,1,0:T(8,128)}, f32[96,768]{1,0:T(8,128)}, f32[96,3072]{1,0:T(8,128)}, f32[384,768]{1,0:T(8,128)}), (f32[1,3,96,768]{3,2,1,0:T(8,128)}, f32[96,768]{1,0:T(8,128)}, f32[96,3072]{1,0:T(8,128)}, ...) | async-done | bytes 3538960 | tf_op jit(solution)/shard_map/psum | solution.py:828
  620.0 2.2 slice_bitcast_fusion
  (55 shorter events, 11.1 us)
Async XLA Ops:
  7.2 180.6 %reduce-scatter.9.cloned.1.call-start = ((), (), s32[]{:S(2)}) async-start(), calls=%async_computation.6 | async-start | bytes 10616832 | tf_op jit(solution)/shard_map/reduce_scatter | solution.py:828
  91.0 1.3 copy-start.2
  91.0 133.6 %reduce-scatter.7.cloned.1.call-start = ((), (), s32[]{:S(2)}) async-start(), calls=%async_computation.5 | async-start | bytes 2654208 | tf_op jit(solution)/shard_map/reduce_scatter | solution.py:828
  93.9 209.7 %reduce-scatter.5.cloned.1.call-start = ((), (), s32[]{:S(2)}) async-start(), calls=%async_computation.4 | async-start | bytes 7962624 | tf_op jit(solution)/shard_map/reduce_scatter | solution.py:828
  158.3 245.4 %reduce-scatter.11.cloned.1.call-start = ((), (), s32[]{:S(2)}) async-start(), calls=%async_computation.7 | async-start | bytes 10616832 | tf_op jit(solution)/shard_map/reduce_scatter | solution.py:828
  165.5 358.4 %all-gather.3.cloned.1.call-start = ((), (), s32[]{:S(2)}) async-start(), calls=%async_computation.8 | async-start | bytes 14155776 | tf_op jit(solution)/shard_map/all_gather | solution.py:842
  166.1 453.9 %all-reduce.3.cloned.1.call-start = ((), (), s32[]{:S(2)}) async-start(), calls=%async_computation.9 | async-start | bytes 7077888 | tf_op jit(solution)/shard_map/psum | solution.py:828
  403.7 1.0 copy-start.6
  403.7 3.9 copy-start.8
  403.7 3.9 copy-start.9
  404.7 121.1 %copy-start = (bf16[2,128,768]{2,1,0:T(8,128)(2,1)S(1)}, bf16[2,128,768]{2,1,0:T(8,128)(2,1)}, u32[]{:S(2)}) copy-start(bf16[2,128,768]{2,1,0:T(8,128)(2,1)} %get-tuple-element.56.xown) | copy-start | bytes 1179652
  404.7 121.1 %copy-start.1 = (f32[256,768]{1,0:T(8,128)S(1)}, f32[256,768]{1,0:T(8,128)}, u32[]{:S(2)}) copy-start(f32[256,768]{1,0:T(8,128)} %get-tuple-element.44) | copy-start | bytes 2359300
  404.7 124.8 %collective-permute-start = (bf16[128,768]{1,0:T(8,128)(2,1)S(1)}, bf16[128,768]{1,0:T(8,128)(2,1)S(1)}, u32[]{:S(2)}, u32[]{:S(2)}) collective-permute-start(bf16[128,768]{1,0:T(8,128)(2,1)S(1)} %get-tuple-element.63), channel_id=1, source_target_pairs={{0,1},{1,0},{2,3},{3,2},{4,5},{5,4},{6,7},{7,6},{8,9},{9,8},{10,11... | collective-permute-start | bytes 589832 | tf_op jit(solution)/shard_map/ppermute | solution.py:853
  525.7 1.1 copy-start.5
  527.2 3.0 collective-permute-start.1
  619.9 2.2 copy-start.7
  619.9 2.9 copy-start.4
  622.1 1.7 copy-start.3
Sparse Core Ops, SparseCore 0:
  91.1 96.6 reduce-scatter.8
  190.1 34.4 reduce-scatter.6
  226.9 76.6 reduce-scatter.4
  305.7 97.8 reduce-scatter.10
  405.2 118.6 all-gather.2
  527.7 92.1 all-reduce.2

commit v2 on v1

--- a/solution.py
+++ b/solution.py
@@ -722,7 +722,7 @@
 
 
 def backward_kernel(
-    xrow, segall, gain, wq, wk, wv, n1, q, k, v, probs, datt, gfin, dpart, dqpart, pqkv, small,
+    xrow, segall, gain, wq, wk, wv, n1, q, k, v, probs, datt, gfin, pout, dpart, dqpart, pqkv, small,
     kaug, dk, dv, dq, near, far, qm, dm, dprob, ds, rows,
 ):
     _, z, c = spot()
@@ -745,6 +745,7 @@
 
     lax.fori_loop(0, probs.shape[0], pair, 0)
     g = gain[...].astype(F32)
+    pqkv[:, 3] = pout[...]
     for i, (left, right) in enumerate(
         ((n1[pl.ds(pl.multiple_of(z * tq, tq), tq), :], dq), (n1[...], dk), (n1[...], dv))
     ):
@@ -773,7 +774,7 @@
     table_sums(near, far, rows, small, 2 * lines, tq)
 
 
-def backward(xrow, segall, gain, wq, wk, wv, n1, q, k, v, probs, datt, gfin):
+def backward(xrow, segall, gain, wq, wk, wv, n1, q, k, v, probs, datt, gfin, pout):
     nb, block, width = xrow.shape
     length, tq = nb * block, 2 * block
     inner = wq.shape[1]
@@ -784,10 +785,10 @@
         out_shape=(
             jax.ShapeDtypeStruct((length // tq, tq, width), BF),
             jax.ShapeDtypeStruct((tq, width), F32),
-            jax.ShapeDtypeStruct((nb, 3, width // nb, inner), BF),
+            jax.ShapeDtypeStruct((nb, 4, width // nb, inner), BF),
             jax.ShapeDtypeStruct((16, TILE), F32),
         ),
-        in_specs=[vm] * 13,
+        in_specs=[vm] * 14,
         out_specs=(vm,) * 4,
         scratch_shapes=[
             pltpu.VMEM((length, TILE), BF),
@@ -803,7 +804,331 @@
             pltpu.VMEM((2 * pairs, 32, TILE), F32),
         ],
         compiler_params=pltpu.CompilerParams(vmem_limit_bytes=VLIMIT),
-    )(xrow, segall, gain, wq, wk, wv, n1, q, k, v, probs, datt, gfin)
+    )(xrow, segall, gain, wq, wk, wv, n1, q, k, v, probs, datt, gfin, pout)
+
+
+class Sums:
+    UNITS = ("down", "in", "attn")
+
+    def __init__(self, nz, bufs, s_sem, r_sem):
+        self.nz = nz
+        self.dp, self.z, self.c = spot()
+        self.bufs, self.s_sem, self.r_sem = bufs, s_sem, r_sem
+        x, y = self.dp % 2, self.dp // 2
+        c = self.c
+        self.f, self.g = 1 + c, 2 - c
+        self.s1 = (1 - c) * x + c * y
+        self.s2 = (1 - c) * y + c * x
+        self.peer1 = self.dp + self.f * (1 - 2 * self.s1)
+        self.peer2 = self.dp + self.g * (1 - 2 * self.s2)
+        self.count = 0
+        self.table = {}
+        self.pending = []
+
+    def sem(self, key):
+        if key not in self.table:
+            self.table[key] = self.count
+            self.count += 1
+        return self.table[key]
+
+    def copy(self, src, dst, key, dp=None, z=None, c=None):
+        n = self.sem(key)
+        dp = self.dp if dp is None else dp
+        z = self.z if z is None else z
+        c = self.c if c is None else c
+        return pltpu.make_async_remote_copy(
+            src, dst, self.s_sem.at[n], self.r_sem.at[n], device_id=(dp, 2 * z + c), device_id_type=MESH
+        )
+
+    def start(self, src, dst, key, **to):
+        op = self.copy(src, dst, key, **to)
+        op.start()
+        self.pending.append(op)
+
+    def drain(self):
+        for op in self.pending:
+            op.wait_send()
+        self.pending = []
+
+    def q(self, i1, i2):
+        return i1 * self.f + i2 * self.g
+
+    def a_start(self, u, zs=None):
+        b = self.bufs[u]
+        for zz in range(self.nz) if zs is None else zs:
+            self.start(b["pb"].at[2 * zz + 1 - self.c], b["ra"].at[zz], (u, "a", zz), c=1 - self.c)
+
+    def a_finish(self, u, zz):
+        b = self.bufs[u]
+        self.copy(b["pb"].at[0], b["ra"].at[zz], (u, "a", zz), c=1 - self.c).wait_recv()
+
+        def one(q, carry):
+            b["ra"][zz, q] = (b["ra"][zz, q].astype(F32) + b["pb"][2 * zz + self.c, q].astype(F32)).astype(BF)
+            return carry
+
+        lax.fori_loop(0, 4, one, 0)
+
+    def first_start(self, u, zz):
+        b = self.bufs[u]
+        for i2 in range(2):
+            self.start(
+                b["ra"].at[zz, self.q(1 - self.s1, i2)], b["r1"].at[zz, i2], (u, "1", zz, i2), dp=self.peer1
+            )
+
+    def first_finish(self, u, zz):
+        b = self.bufs[u]
+        for i2 in range(2):
+            self.copy(b["ra"].at[0, 0], b["r1"].at[zz, i2], (u, "1", zz, i2)).wait_recv()
+            b["r1"][zz, i2] = (
+                b["r1"][zz, i2].astype(F32) + b["ra"][zz, self.q(self.s1, i2)].astype(F32)
+            ).astype(BF)
+
+    def second_start(self, u, zz):
+        b = self.bufs[u]
+        self.start(b["r1"].at[zz, 1 - self.s2], b["r2"].at[zz], (u, "2", zz), dp=self.peer2)
+
+    def second_finish(self, u, zz):
+        b = self.bufs[u]
+        self.copy(b["r1"].at[0, 0], b["r2"].at[zz], (u, "2", zz)).wait_recv()
+        b["r2"][zz] = (b["r2"][zz].astype(F32) + b["r1"][zz, self.s2].astype(F32)).astype(BF)
+
+    def z_start(self, u, name):
+        b = self.bufs[u]
+        for dz in range(1, self.nz):
+            to = lax.rem(self.z + dz, self.nz)
+            self.start(b[name].at[to], b["rz"].at[self.nz - 1 - dz], (u, "z", self.nz - 1 - dz), z=to)
+
+    def z_wait(self, u, name):
+        b = self.bufs[u]
+        for slot in range(self.nz - 1):
+            self.copy(b[name].at[0], b["rz"].at[slot], (u, "z", slot)).wait_recv()
+
+    def z_finish_last(self, u):
+        self.z_wait(u, "r2")
+        b = self.bufs[u]
+        total = b["r2"][self.z].astype(F32)
+        for slot in range(self.nz - 1):
+            total = total + b["rz"][slot].astype(F32)
+        b["g"][self.dp] = total.astype(BF)
+
+    def z_finish_mid(self, u):
+        self.z_wait(u, "r1")
+        b = self.bufs[u]
+        for i2 in range(2):
+            total = b["r1"][self.z, i2].astype(F32)
+            for slot in range(self.nz - 1):
+                total = total + b["rz"][slot, i2].astype(F32)
+            b["r1"][self.z, i2] = total.astype(BF)
+
+    def second_last_start(self, u):
+        b = self.bufs[u]
+        self.start(b["r1"].at[self.z, 1 - self.s2], b["r2"].at[0], (u, "2", 0), dp=self.peer2)
+
+    def second_last_finish(self, u):
+        b = self.bufs[u]
+        self.copy(b["r1"].at[0, 0], b["r2"].at[0], (u, "2", 0)).wait_recv()
+        total = b["r2"][0].astype(F32) + b["r1"][self.z, self.s2].astype(F32)
+        b["g"][self.dp] = total.astype(BF)
+
+    def spread_start(self, u):
+        b = self.bufs[u]
+        for k in range(1, 4):
+            self.start(
+                b["g"].at[self.dp], b["g"].at[self.dp], (u, "g", 3 - k), dp=lax.rem(self.dp + k, 4)
+            )
+
+    def spread_finish(self, u):
+        b = self.bufs[u]
+        for k in range(1, 4):
+            self.copy(b["g"].at[0], b["g"].at[lax.rem(self.dp + k, 4)], (u, "g", 3 - (4 - k))).wait_recv()
+
+
+def unit_scratch(nz, share, width, order):
+    block = (share, width)
+    return {
+        "ra": pltpu.VMEM((nz, 4) + block, BF),
+        "r1": pltpu.VMEM((nz, 2) + block, BF),
+        "r2": pltpu.VMEM(((nz,) if order == "xyz" else (1,)) + block, BF),
+        "rz": pltpu.VMEM((nz - 1,) + (() if order == "xyz" else (2,)) + block, BF),
+        "g": pltpu.VMEM((4,) + block, BF),
+    }
+
+
+def reduce_kernel(nz, names, *refs):
+    pdown, pin, pattn, small, dpart, dqpart, xown, dh, gain, out_own = refs[:10]
+    o_out, o_gt, o_down, o_in, o_q, o_k, o_v, o_o, o_small = refs[10:19]
+    scr = list(refs[19:])
+    bufs = {}
+    for u, part in (("down", pdown), ("in", pin), ("attn", pattn)):
+        bufs[u] = {"pb": part}
+        for name in names:
+            bufs[u][name] = scr.pop(0)
+    rd, gt, sm, smr, s_sem, r_sem, l_sem = scr
+    eng = Sums(nz, bufs, s_sem, r_sem)
+    dp, z, c = eng.dp, eng.z, eng.c
+    barrier = pltpu.get_barrier_semaphore()
+    peers = [(dp, 2 * z + 1 - c)]
+    peers += [(lax.rem(dp + k, 4), 2 * z + c) for k in range(1, 4)]
+    peers += [(dp, 2 * lax.rem(z + k, nz) + c) for k in range(1, nz)]
+    for peer in peers:
+        pl.semaphore_signal(barrier, inc=1, device_id=peer, device_id_type=MESH)
+    pl.semaphore_wait(barrier, len(peers))
+
+    for u in Sums.UNITS:
+        eng.a_start(u)
+    tq, width = dqpart.shape
+    reach = -(-REACH // tq)
+
+    def near(other):
+        return jnp.abs(other - z) <= reach
+
+    for dz in range(1, nz):
+        to = lax.rem(z + dz, nz)
+        op = eng.copy(dpart.at[to], rd.at[nz - 1 - dz], ("d", nz - 1 - dz), z=to)
+
+        @pl.when(near(to))
+        def _():
+            op.start()
+
+    eng.start(out_own.at[1 - c], o_out.at[c], ("out",), c=1 - c)
+    kept = pltpu.make_async_copy(out_own.at[c], o_out.at[c], l_sem.at[0])
+    kept.start()
+
+    hops = (dict(c=1 - c), dict(dp=dp + 1 - 2 * (dp % 2)), dict(dp=dp + 2 - 4 * (dp // 2)),
+            dict(z=z + 1 - 2 * (z % 2)), dict(z=z + 2 - 4 * (z // 2)))
+    sm[0] = small[...]
+
+    def small_start(i):
+        eng.start(sm.at[i], smr.at[i], ("s", i), **hops[i])
+
+    def small_finish(i):
+        eng.copy(sm.at[i], smr.at[i], ("s", i), **hops[i]).wait_recv()
+        sm[i + 1] = sm[i] + smr[i]
+
+    small_start(0)
+    for zz in range(nz):
+        eng.a_finish("down", zz)
+        eng.first_start("down", zz)
+    small_finish(0)
+    small_start(1)
+    for zz in range(nz):
+        eng.a_finish("in", zz)
+        eng.first_start("in", zz)
+    for zz in range(nz):
+        eng.a_finish("attn", zz)
+        eng.first_start("attn", zz)
+    small_finish(1)
+    small_start(2)
+    for zz in range(nz):
+        eng.first_finish("down", zz)
+    eng.z_start("down", "r1")
+    for zz in range(nz):
+        eng.first_finish("in", zz)
+        eng.second_start("in", zz)
+    small_finish(2)
+    small_start(3)
+    for zz in range(nz):
+        eng.first_finish("attn", zz)
+        eng.second_start("attn", zz)
+    eng.z_finish_mid("down")
+    eng.second_last_start("down")
+    for zz in range(nz):
+        eng.second_finish("in", zz)
+    eng.z_start("in", "r2")
+    small_finish(3)
+    small_start(4)
+    eng.second_last_finish("down")
+    eng.spread_start("down")
+    for zz in range(nz):
+        eng.second_finish("attn", zz)
+    eng.z_start("attn", "r2")
+    eng.z_finish_last("in")
+    eng.spread_start("in")
+
+    for slot in range(nz - 1):
+        src = lax.rem(z + slot + 1, nz)
+
+        @pl.when(near(src))
+        def _():
+            eng.copy(dpart.at[0], rd.at[slot], ("d", slot)).wait_recv()
+
+        @pl.when(jnp.logical_not(near(src)))
+        def _():
+            rd[slot] = jnp.zeros((tq, width), BF)
+
+    g = gain[...].astype(F32)
+    dn1 = dqpart[...]
+    for slot in range(nz - 1):
+        dn1 = dn1 + rd[slot].astype(F32)
+    normed, scale, _ = norm_rows(xown[...].reshape(tq, width), g)
+    back, _ = rms_backward(dn1, normed, scale, g)
+    gt[...] = (dh[...] + back).astype(BF).reshape(gt.shape)
+    eng.start(gt.at[1 - c], o_gt.at[c], ("gt",), c=1 - c)
+    kept_gt = pltpu.make_async_copy(gt.at[c], o_gt.at[c], l_sem.at[1])
+    kept_gt.start()
+
+    eng.z_finish_last("attn")
+    eng.spread_start("attn")
+    small_finish(4)
+    o_small[...] = sm[5]
+    eng.spread_finish("down")
+    o_down[...] = bufs["down"]["g"][...].astype(F32)
+    eng.spread_finish("in")
+    for j in range(4):
+        o_in[:, j * width : (j + 1) * width] = bufs["in"]["g"][j].astype(F32)
+    eng.spread_finish("attn")
+    for j, ref in enumerate((o_q, o_k, o_v, o_o)):
+        ref[...] = bufs["attn"]["g"][j].astype(F32)
+    eng.copy(out_own.at[0], o_out.at[1 - c], ("out",)).wait_recv()
+    eng.copy(gt.at[0], o_gt.at[1 - c], ("gt",)).wait_recv()
+    kept.wait()
+    kept_gt.wait()
+    eng.drain()
+    for dz in range(1, nz):
+        to = lax.rem(z + dz, nz)
+
+        @pl.when(near(to))
+        def _():
+            eng.copy(dpart.at[to], rd.at[nz - 1 - dz], ("d", nz - 1 - dz), z=to).wait_send()
+
+
+def reduce(nz, pdown, pin, pattn, small, dpart, dqpart, xown, dh, gain, out_own):
+    nb, _, share, width = pattn.shape
+    tq = dqpart.shape[0]
+    names = ("ra", "r1", "r2", "rz", "g")
+    scratch = []
+    for u in Sums.UNITS:
+        bufs = unit_scratch(nz, share, width, "xzy" if u == "down" else "xyz")
+        scratch += [bufs[name] for name in names]
+    vm = pl.BlockSpec(memory_space=pltpu.VMEM)
+    home = jax.ShapeDtypeStruct((2, tq // 2, width), BF)
+    one = jax.ShapeDtypeStruct((share, width), F32)
+    return pl.pallas_call(
+        functools.partial(reduce_kernel, nz, names),
+        out_shape=(
+            home,
+            home,
+            jax.ShapeDtypeStruct((4, share, width), F32),
+            jax.ShapeDtypeStruct((share, 4 * width), F32),
+            one, one, one, one,
+            jax.ShapeDtypeStruct(small.shape, F32),
+        ),
+        in_specs=[vm] * 10,
+        out_specs=(vm,) * 9,
+        scratch_shapes=scratch
+        + [
+            pltpu.VMEM((nz - 1, tq, width), BF),
+            pltpu.VMEM((2, tq // 2, width), BF),
+            pltpu.VMEM((6,) + small.shape, F32),
+            pltpu.VMEM((5,) + small.shape, F32),
+            pltpu.SemaphoreType.DMA((96,)),
+            pltpu.SemaphoreType.DMA((96,)),
+            pltpu.SemaphoreType.DMA((2,)),
+        ],
+        compiler_params=pltpu.CompilerParams(
+            collective_id=2, has_side_effects=True, vmem_limit_bytes=VLIMIT
+        ),
+    )(pdown, pin, pattn, small, dpart, dqpart, xown, dh, gain, out_own)
 
 
 def fast_device(
@@ -812,7 +1137,6 @@
 ):
     rows, block, width = tokens.shape
     nb, quarters = 2 * nz, 4
-    tq = 2 * block
     z, c = lax.axis_index("blk") // 2, lax.axis_index("blk") % 2
     xrow, dyrow, segall = gather(nz, tokens, cotangent, segment_ids)
     g1, g2 = gain_attn.reshape(1, width), gain_ffn.reshape(1, width)
@@ -821,17 +1145,13 @@
     out, dh, datt, pdown, pin, pout, gfin = ffn(
         xown, att, dyrow, g2, w_out, w_in, w_down, nb, quarters
     )
-    dpart, dqpart, pqkv, small = backward(
-        xrow, segall, g1, w_query, w_key, w_value, n1, q, k, v, probs, datt, gfin
-    )
-    def scatter(part):
-        return lax.psum(lax.psum_scatter(part.astype(F32), "blk", tiled=True), "dp")[0]
-
-    gdown = scatter(pdown).reshape(-1, width)
-    gin = jnp.transpose(scatter(pin), (1, 0, 2)).reshape(width // nb, -1)
-    gqkv = scatter(pqkv)
-    gout = scatter(pout)
-    flat = lax.psum(small, ("dp", "blk")).reshape(-1)
+    dpart, dqpart, pattn, small = backward(
+        xrow, segall, g1, w_query, w_key, w_value, n1, q, k, v, probs, datt, gfin, pout
+    )
+    out, grad_tokens, gdown, gin, gq, gk, gv, go, small = reduce(
+        nz, pdown, pin, pattn, small, dpart, dqpart, xown, dh, g1, out
+    )
+    flat = small.reshape(-1)
     b = lax.axis_index("blk")
     share = width // nb
     ga = lax.dynamic_slice_in_dim(flat[:width], b * share, share)
@@ -839,24 +1159,7 @@
     heads = rel_table.shape[1]
     gt = flat[2 * width : 2 * width + 32 * heads].reshape(heads, 32).T
     gt = lax.dynamic_slice_in_dim(gt, b * (32 // nb), 32 // nb)
-    every = lax.all_gather(dpart, "blk", axis=0).reshape(nz, 2, nz, tq, width)
-    mine = every[:, c][:, z].astype(F32)
-    keep = (jnp.arange(nz) != z)[:, None, None]
-    dn1 = dqpart + jnp.sum(jnp.where(keep, mine, 0.0), axis=0)
-    x = xown.reshape(tq, width).astype(F32)
-    normed, scale, _ = rms_forward(x, gain_attn.astype(F32))
-    back, _ = rms_backward(dn1, normed, scale, gain_attn.astype(F32))
-    grad_tokens = (dh + back).astype(BF).reshape(2, block, width)
-
-    def home(own):
-        pairs = [(i, i ^ 1) for i in range(nb)]
-        other = lax.ppermute(lax.dynamic_index_in_dim(own, 1 - c, 0, False), "blk", pairs)
-        kept = lax.dynamic_index_in_dim(own, c, 0, False)
-        return jnp.where(c == 0, jnp.stack([kept, other]), jnp.stack([other, kept]))
-
-    return (
-        home(out), home(grad_tokens), ga, gqkv[0], gqkv[1], gqkv[2], gout, gf, gin, gdown, gt,
-    )
+    return (out, grad_tokens, ga, gq, gk, gv, go, gf, gin, gdown.reshape(-1, width), gt)
 
 
 def pick(mesh):

time: 634 us -> 245 us (0.39)
  waiting for transfers between devices: 401 us -> 0 us
  Pallas kernels: 128 us -> 227 us
  blocking collectives: 40.3 us -> 0 us
  other arithmetic: 27.5 us -> 0 us
  between operations: 14.2 us -> 0.74 us
    reduce_scatter x4 -> x0, waiting for transfers between devices: 235 us -> none  [scatter(): lax.psum_scatter(part.astype(F32), 'blk', tiled=True)]
    pallas_call x0 -> x1, Pallas kernels: none -> 99.3 us  [reduce(): pl.pallas_call(functools.partial(reduce_kernel, nz, names), out_shape=(ho...]
    psum x1 -> x0, waiting for transfers between devices: 88.9 us -> none  [scatter(): lax.psum(lax.psum_scatter(part.astype(F32), 'blk', tiled=True), 'dp')[0]]
    all_gather x1 -> x0, waiting for transfers between devices: 75.9 us -> none  [fast_device(): every = lax.all_gather(dpart, 'blk', axis=0).reshape(nz, 2, nz, tq, width)]
    psum x1 -> x0, blocking collectives: 40.3 us -> none  [fast_device(): flat = lax.psum(small, ('dp', 'blk')).reshape(-1)]
    convert_element_type x6 -> x0, other arithmetic: 21.9 us -> none  [the longest x4 21.6 us: scatter(): part.astype(F32)]
  transfers between devices with their start and end apart: 8 -> 0, of which waited for: 6 -> 0; matrix products, arithmetic and copies ran while one was open for 4% -> 0% of each run, Pallas kernels for 9% -> 0%
where the time goes in v2:
time: 245 us; the launch traced here: 244 us
  Pallas kernels  227 us (93%)
  local copies, waits for them, and re-layouts  16.4 us (7%)
    pallas_call x1, Pallas kernels, reduce(): pl.pallas_call(functools.partial(reduce_kernel, nz, names), out_shape=(ho...  99.3 us
    pallas_call x1, Pallas kernels, backward(): pl.pallas_call(backward_kernel, out_shape=(jax.ShapeDtypeStruct((length /...  58.3 us
    pallas_call x1, Pallas kernels, forward(): pl.pallas_call(forward_kernel, out_shape=(jax.ShapeDtypeStruct((length, w...  28.2 us
    pallas_call x1, Pallas kernels, gather(): pl.pallas_call(functools.partial(gather_kernel, nz), out_shape=(jax.Shape...  25.7 us
    pallas_call x1, Pallas kernels, ffn(): pl.pallas_call(ffn_kernel, out_shape=(jax.ShapeDtypeStruct((2, tq // 2, w...  15.7 us
    unnamed x28, local copies, waits for them, and re-layouts  9.95 us

profile of v2, /device:TPU:3, one launch (start us, length us, event | category | flops | bytes accessed | tf_op | source)
XLA Modules:
  0.0 244.4 jit_solution(7600092179981244527)
XLA Ops:
  0.7 25.7 %shard_map.203 = (bf16[8,128,768]{2,1,0:T(8,128)(2,1)}, bf16[2,128,768]{2,1,0:T(8,128)(2,1)}, s32[8,8,128]{2,1,0:T(8,128)}) custom-call(bf16[2,128,768]{2,1,0:T(8,128)(2,1)} %tok.1, bf16[2,128,768]{2,1,0:T(8,128)(2,1)} %dy.1, s32[2,128]{1,0:T(2,128)} %seg.1), custom_call_target="tpu_custom_call" | custom-call | tf_op jit(solution)/shard_map/pallas_call | solution.py:395
  26.4 1.8 constant_dynamic-slice_fusion.1.xown.refs_6_
  28.2 0.6 reshape.39.gain.refs_8_
  28.8 0.7 copy.27.ts
  29.5 0.7 copy.26.table
  30.2 28.2 %shard_map.204 = (bf16[1024,768]{1,0:T(8,128)(2,1)}, bf16[1024,768]{1,0:T(8,128)(2,1)}, bf16[1024,768]{1,0:T(8,128)(2,1)}, bf16[256,768]{1,0:T(8,128)(2,1)}, bf1...) custom-call(bf16[8,128,768]{2,1,0:T(8,128)(2,1)} %get-tuple-element.40.xrow, s32[8,8,128]{2,1,0:T(8,128)} %get-tuple-element.41.segall, ...), custom_call_target="tpu_custom_call" | custom-call | tf_op jit(solution)/shard_map/pallas_call | solution.py:551
  58.4 0.6 reshape.40.gain
  58.9 15.7 %shard_map.205 = (bf16[2,128,768]{2,1,0:T(8,128)(2,1)}, f32[256,768]{1,0:T(8,128)}, bf16[256,768]{1,0:T(8,128)(2,1)}, bf16[8,4,96,768]{3,2,1,0:T(8,128)(2,1)}, b...) custom-call(bf16[2,128,768]{2,1,0:T(8,128)(2,1)} %constant_dynamic-slice_fusion.1.xown.refs_6_, ...), custom_call_target="tpu_custom_call" | custom-call | tf_op jit(solution)/shard_map/pallas_call | solution.py:624
  74.7 58.3 %shard_map.206 = (bf16[4,256,768]{2,1,0:T(8,128)(2,1)}, f32[256,768]{1,0:T(8,128)}, bf16[8,4,96,768]{3,2,1,0:T(8,128)(2,1)}, f32[16,128]{1,0:T(8,128)}) custom-call(bf16[8,128,768]{2,1,0:T(8,128)(2,1)} %get-tuple-element.40.xrow, s32[8,8,128]{2,1,0:T(8,128)} %get-tuple-element.41.segall, bf16[1,768]{1,0:T(2,128)(2,1)} %reshape.39.gain.refs_8_, ...), custom_call_target="tpu_custom_call" | custom-call | tf_op jit(solution)/shard_map/pallas_call | solution.py:783
  133.0 99.3 %shard_map.207 = (bf16[2,128,768]{2,1,0:T(8,128)(2,1)}, bf16[2,128,768]{2,1,0:T(8,128)(2,1)}, f32[4,96,768]{2,1,0:T(8,128)}, f32[96,3072]{1,0:T(8,128)}, f32[96,...) custom-call(bf16[8,4,96,768]{3,2,1,0:T(8,128)(2,1)} %get-tuple-element.44.refs, ...), custom_call_target="tpu_custom_call" | custom-call | tf_op jit(solution)/shard_map/pallas_call | solution.py:1106
  232.4 0.8 slice.20
  233.1 0.1 reshape.42
  233.3 0.7 copy.29
  233.9 0.8 slice_bitcast_fusion
  234.7 0.6 dynamic_slice.13
  235.3 0.6 dynamic_slice.14
  235.9 1.8 copy.38
  237.7 1.9 copy.39
  239.5 0.7 copy.40
  240.3 0.7 copy.41
  241.0 0.7 copy.42
  241.7 0.7 copy.43
  242.4 1.0 copy.44
  243.4 1.0 copy.45
  (19 shorter events, 0.1 us)
Async XLA Ops:
  0.6 27.5 %copy-start.7 = (bf16[768]{0:T(1024)(128)(2,1)S(1)}, bf16[768]{0:T(1024)(128)(2,1)}, u32[]{:S(2)}) copy-start(bf16[768]{0:T(1024)(128)(2,1)} %param.14) | copy-start | bytes 4612
  0.7 28.1 %copy-start.6 = (bf16[32,12]{0,1:T(8,128)(2,1)S(1)}, bf16[32,12]{0,1:T(8,128)(2,1)}, u32[]{:S(2)}) copy-start(bf16[32,12]{0,1:T(8,128)(2,1)} %param.22) | copy-start | bytes 2308
  30.2 28.2 %copy-start.8 = (bf16[768]{0:T(1024)(128)(2,1)S(1)}, bf16[768]{0:T(1024)(128)(2,1)}, u32[]{:S(2)}) copy-start(bf16[768]{0:T(1024)(128)(2,1)} %param.19) | copy-start | bytes 4612
  232.3 7.2 %copy-start.5 = (f32[96,768]{1,0:T(8,128)S(1)}, f32[96,768]{1,0:T(8,128)}, u32[]{:S(2)}) copy-start(f32[96,768]{1,0:T(8,128)} %get-tuple-element.85) | copy-start | bytes 884740
  232.3 7.9 %copy-start.4 = (f32[96,768]{1,0:T(8,128)S(1)}, f32[96,768]{1,0:T(8,128)}, u32[]{:S(2)}) copy-start(f32[96,768]{1,0:T(8,128)} %get-tuple-element.86) | copy-start | bytes 884740
  232.3 8.6 %copy-start.3 = (f32[96,768]{1,0:T(8,128)S(1)}, f32[96,768]{1,0:T(8,128)}, u32[]{:S(2)}) copy-start(f32[96,768]{1,0:T(8,128)} %get-tuple-element.87) | copy-start | bytes 884740
  235.9 5.8 %copy-start.2 = (f32[96,768]{1,0:T(8,128)S(1)}, f32[96,768]{1,0:T(8,128)}, u32[]{:S(2)}) copy-start(f32[96,768]{1,0:T(8,128)} %get-tuple-element.88) | copy-start | bytes 884740
  237.7 4.7 %copy-start.1 = (f32[96,3072]{1,0:T(8,128)S(1)}, f32[96,3072]{1,0:T(8,128)}, u32[]{:S(2)}) copy-start(f32[96,3072]{1,0:T(8,128)} %get-tuple-element.90) | copy-start | bytes 3538948
  241.7 1.7 copy-start
